TPU v7x, 128 devices: a whole 4x4x4 slice. The times are simulated.
128 devices in a mesh: ctx: 128 (over z, x, y, core).
Axes of the slice: x: 4, y: 4, z: 4, core: 2. Of those that a mesh axis runs over, the one named last changes fastest.
Arguments:
- q_noised: bfloat16 [32768, 2048], P('ctx'), may hold values from -6 to 6
- k_noised: bfloat16 [32768, 2048], P('ctx'), may hold values from -6 to 6
- v_noised: bfloat16 [32768, 2048], P('ctx'), may hold values from -6 to 6
- dout: bfloat16 [32768, 2048], P('ctx'), may hold values from -6 to 6
- lse: float32 [16, 32768], P(None, 'ctx'), may hold values from 7.5 to 9
- delta: float32 [16, 32768], P(None, 'ctx'), may hold values from -48 to 48
- listed: int32 [128, 8], P('ctx'), may hold values from 0 to 255, as said below
- k_clean: bfloat16 [65536, 2048], P('ctx'), may hold values from -6 to 6
- v_clean: bfloat16 [65536, 2048], P('ctx'), may hold values from -6 to 6
Outputs:
- dq: bfloat16 [32768, 2048], P('ctx')
- dk_noised: bfloat16 [32768, 2048], P('ctx')
- dv_noised: bfloat16 [32768, 2048], P('ctx')
- dk_clean: bfloat16 [65536, 2048], P('ctx')
- dv_clean: bfloat16 [65536, 2048], P('ctx')
Inputs may be any that keep to these rules, and one draw needn't show every extreme that they name: Row b lists 8 distinct clean blocks, each among the 16 clean blocks c with (b - 1 - c // 2) mod 128 < 8; how often a clean block is listed varies.
All inputs are finite; a program needn't handle non-finite values.
Results may differ from a plain program's by a relative error of at most 0.0053.
Values may be sent and summed in bfloat16 or wider, within the bound.
A program may use at most 384 MiB of HBM per device.

v0:
```python
import jax
import jax.numpy as jnp
from jax import lax
from jax.sharding import PartitionSpec as P

CLEAN_DEV = 2
REACH = 8


def from_behind(value, axis, steps):
    count = lax.axis_size(axis)
    pairs = [(source, (source + steps) % count) for source in range(count)]
    return lax.ppermute(value, axis, pairs)


def pair_grads(query, grad_out, log_sums, deltas, keys, values, weight):
    rows = query.shape[0]
    heads = log_sums.shape[0]
    size = query.shape[1] // heads
    scale = size ** (-0.5)
    q_heads = query.reshape(rows, heads, size)
    o_heads = grad_out.reshape(rows, heads, size)
    k_heads = keys.reshape(keys.shape[0], heads, size)
    v_heads = values.reshape(values.shape[0], heads, size)
    scores = (
        jnp.einsum("qhd,khd->hqk", q_heads, k_heads, preferred_element_type=jnp.float32) * scale
    )
    probs = jnp.exp(scores - log_sums[:, :, None]) * weight
    probs_low = probs.astype(jnp.bfloat16)
    grad_v = jnp.einsum("hqk,qhd->khd", probs_low, o_heads, preferred_element_type=jnp.float32)
    grad_p = jnp.einsum("qhd,khd->hqk", o_heads, v_heads, preferred_element_type=jnp.float32)
    grad_s = (probs * (grad_p - deltas[:, :, None])).astype(jnp.bfloat16)
    grad_q = jnp.einsum("hqk,khd->qhd", grad_s, k_heads, preferred_element_type=jnp.float32) * scale
    grad_k = jnp.einsum("hqk,qhd->khd", grad_s, q_heads, preferred_element_type=jnp.float32) * scale
    width = query.shape[1]
    return (
        grad_q.reshape(rows, width),
        grad_k.reshape(keys.shape[0], width),
        grad_v.reshape(keys.shape[0], width),
    )


def visit(query, grad_out, log_sums, deltas, ids, k_clean, v_clean, first_id):
    rows = query.shape[0]
    width = query.shape[1]
    part_q = jnp.zeros((rows, width), jnp.float32)
    keys_grads = []
    values_grads = []
    for slot in range(CLEAN_DEV):
        keys = k_clean[slot * rows : (slot + 1) * rows]
        values = v_clean[slot * rows : (slot + 1) * rows]
        flag = jnp.any(ids == first_id + slot)
        grads = pair_grads(
            query, grad_out, log_sums, deltas, keys, values, flag.astype(jnp.float32)
        )
        part_q = part_q + grads[0]
        keys_grads.append(grads[1])
        values_grads.append(grads[2])
    return (part_q, jnp.concatenate(keys_grads, axis=0), jnp.concatenate(values_grads, axis=0))


def per_device(q_noised, k_noised, v_noised, dout, lse, delta, listed, k_clean, v_clean):
    first_id = lax.axis_index("ctx") * CLEAN_DEV
    own_q, own_k, own_v = pair_grads(q_noised, dout, lse, delta, k_noised, v_noised, 1.0)
    clean_k = jnp.zeros(k_clean.shape, jnp.float32)
    clean_v = jnp.zeros(v_clean.shape, jnp.float32)

    def cycle_step(step, carry):
        query, grad_out, log_sums, deltas, ids, acc_q, acc_k, acc_v = carry
        query, grad_out = from_behind((query, grad_out), "ctx", -1)
        log_sums, deltas, acc_q = from_behind((log_sums, deltas, acc_q), "ctx", -1)
        ids = from_behind(ids, "ctx", -1)
        part_q, part_k, part_v = visit(
            query, grad_out, log_sums, deltas, ids, k_clean, v_clean, first_id
        )
        return (
            query,
            grad_out,
            log_sums,
            deltas,
            ids,
            acc_q + part_q,
            acc_k + part_k,
            acc_v + part_v,
        )

    start_q = jnp.zeros(own_q.shape, jnp.float32)
    carry = lax.fori_loop(
        0, REACH, cycle_step, (q_noised, dout, lse, delta, listed, start_q, clean_k, clean_v)
    )
    clean_k = carry[6]
    clean_v = carry[7]
    total_q = own_q + from_behind(carry[5], "ctx", REACH)
    return (
        total_q.astype(jnp.bfloat16),
        own_k.astype(jnp.bfloat16),
        own_v.astype(jnp.bfloat16),
        clean_k.astype(jnp.bfloat16),
        clean_v.astype(jnp.bfloat16),
    )


def solution(mesh):
    placed = (
        P("ctx", None),
        P("ctx", None),
        P("ctx", None),
        P("ctx", None),
        P(None, "ctx"),
        P(None, "ctx"),
        P("ctx", None),
        P("ctx", None),
        P("ctx", None),
    )
    return jax.shard_map(
        per_device,
        mesh=mesh,
        in_specs=placed,
        out_specs=(P("ctx", None), P("ctx", None), P("ctx", None), P("ctx", None), P("ctx", None)),
        check_vma=False,
    )
```

profile of v0, /device:TPU:1, one launch (start us, length us, event | category | flops | bytes accessed | tf_op | source)
XLA Modules:
  0.0 531.0 jit_solution(17818973244406508541)
XLA Ops:
  6.2 4.0 copy.48
  10.2 4.0 copy.49
  14.1 461.2 %while.26 = (s32[]{:T(128)}, bf16[256,2048]{0,1:T(8,128)(2,1)}, bf16[256,2048]{0,1:T(8,128)(2,1)}, f32[16,256]{1,0:T(8,128)S(1)}, f32[16,256]{1,0:T(8,128)S(1)},...) while((s32[]{:T(128)}, bf16[256,2048]{0,1:T(8,128)(2,1)}, ...), condition=%wide.region_3.0_spmd.clone, body=%wide.region_0.0_spmd.clone.sunk | while | flops 2714763264 | bytes 224691088 | solution.py:88
  15.6 8.2 %collective-permute-start.3 = (f32[16,256]{1,0:T(8,128)S(1)}, f32[16,256]{1,0:T(8,128)S(1)}, u32[]{:S(2)}, u32[]{:S(2)}) collective-permute-start(f32[16,256]{1,0:T(8,128)S(1)} %get-tuple-element.334), channel_id=1, source_target_pairs={{0,127},{1,0},{2,1},{3,2},{4,3},{5,4},{6,5},{7,6},{8,7},{9,8},{10,... | collective-permute-start | bytes 49160 | tf_op jit(solution)/shard_map/while/body/eval_jaxpr/ppermute | solution.py:13
  25.4 4.4 fusion.104
  33.1 17.1 %collective-permute-done = bf16[256,2048]{0,1:T(8,128)(2,1)S(1)} collective-permute-done((bf16[256,2048]{0,1:T(8,128)(2,1)}, bf16[256,2048]{0,1:T(8,128)(2,1)S(1)}, u32[]{:S(2)}, u32[]{:S(2)}) %collective-permute-start) | collective-permute-done | bytes 1048608 | tf_op jit(solution)/shard_map/while/body/eval_jaxpr/ppermute | solution.py:13
  69.7 3.1 collective-permute-done.5
  72.8 3.1 bitcast_add_fusion.2
  75.9 6.3 %collective-permute-start.3 = (f32[16,256]{1,0:T(8,128)S(1)}, f32[16,256]{1,0:T(8,128)S(1)}, u32[]{:S(2)}, u32[]{:S(2)}) collective-permute-start(f32[16,256]{1,0:T(8,128)S(1)} %get-tuple-element.334), channel_id=1, source_target_pairs={{0,127},{1,0},{2,1},{3,2},{4,3},{5,4},{6,5},{7,6},{8,7},{9,8},{10,... | collective-permute-start | bytes 49160 | tf_op jit(solution)/shard_map/while/body/eval_jaxpr/ppermute | solution.py:13
  82.3 4.4 fusion.104
  90.1 17.8 %collective-permute-done = bf16[256,2048]{0,1:T(8,128)(2,1)S(1)} collective-permute-done((bf16[256,2048]{0,1:T(8,128)(2,1)}, bf16[256,2048]{0,1:T(8,128)(2,1)S(1)}, u32[]{:S(2)}, u32[]{:S(2)}) %collective-permute-start) | collective-permute-done | bytes 1048608 | tf_op jit(solution)/shard_map/while/body/eval_jaxpr/ppermute | solution.py:13
  127.4 3.1 collective-permute-done.5
  130.5 3.1 bitcast_add_fusion.2
  133.6 5.6 %collective-permute-start.3 = (f32[16,256]{1,0:T(8,128)S(1)}, f32[16,256]{1,0:T(8,128)S(1)}, u32[]{:S(2)}, u32[]{:S(2)}) collective-permute-start(f32[16,256]{1,0:T(8,128)S(1)} %get-tuple-element.334), channel_id=1, source_target_pairs={{0,127},{1,0},{2,1},{3,2},{4,3},{5,4},{6,5},{7,6},{8,7},{9,8},{10,... | collective-permute-start | bytes 49160 | tf_op jit(solution)/shard_map/while/body/eval_jaxpr/ppermute | solution.py:13
  139.3 4.4 fusion.104
  147.0 17.8 %collective-permute-done = bf16[256,2048]{0,1:T(8,128)(2,1)S(1)} collective-permute-done((bf16[256,2048]{0,1:T(8,128)(2,1)}, bf16[256,2048]{0,1:T(8,128)(2,1)S(1)}, u32[]{:S(2)}, u32[]{:S(2)}) %collective-permute-start) | collective-permute-done | bytes 1048608 | tf_op jit(solution)/shard_map/while/body/eval_jaxpr/ppermute | solution.py:13
  184.4 3.1 collective-permute-done.5
  187.4 3.1 bitcast_add_fusion.2
  190.5 5.6 %collective-permute-start.3 = (f32[16,256]{1,0:T(8,128)S(1)}, f32[16,256]{1,0:T(8,128)S(1)}, u32[]{:S(2)}, u32[]{:S(2)}) collective-permute-start(f32[16,256]{1,0:T(8,128)S(1)} %get-tuple-element.334), channel_id=1, source_target_pairs={{0,127},{1,0},{2,1},{3,2},{4,3},{5,4},{6,5},{7,6},{8,7},{9,8},{10,... | collective-permute-start | bytes 49160 | tf_op jit(solution)/shard_map/while/body/eval_jaxpr/ppermute | solution.py:13
  196.2 4.4 fusion.104
  204.0 17.8 %collective-permute-done = bf16[256,2048]{0,1:T(8,128)(2,1)S(1)} collective-permute-done((bf16[256,2048]{0,1:T(8,128)(2,1)}, bf16[256,2048]{0,1:T(8,128)(2,1)S(1)}, u32[]{:S(2)}, u32[]{:S(2)}) %collective-permute-start) | collective-permute-done | bytes 1048608 | tf_op jit(solution)/shard_map/while/body/eval_jaxpr/ppermute | solution.py:13
  241.3 3.1 collective-permute-done.5
  244.4 3.1 bitcast_add_fusion.2
  247.5 5.6 %collective-permute-start.3 = (f32[16,256]{1,0:T(8,128)S(1)}, f32[16,256]{1,0:T(8,128)S(1)}, u32[]{:S(2)}, u32[]{:S(2)}) collective-permute-start(f32[16,256]{1,0:T(8,128)S(1)} %get-tuple-element.334), channel_id=1, source_target_pairs={{0,127},{1,0},{2,1},{3,2},{4,3},{5,4},{6,5},{7,6},{8,7},{9,8},{10,... | collective-permute-start | bytes 49160 | tf_op jit(solution)/shard_map/while/body/eval_jaxpr/ppermute | solution.py:13
  253.2 4.4 fusion.104
  260.9 17.8 %collective-permute-done = bf16[256,2048]{0,1:T(8,128)(2,1)S(1)} collective-permute-done((bf16[256,2048]{0,1:T(8,128)(2,1)}, bf16[256,2048]{0,1:T(8,128)(2,1)S(1)}, u32[]{:S(2)}, u32[]{:S(2)}) %collective-permute-start) | collective-permute-done | bytes 1048608 | tf_op jit(solution)/shard_map/while/body/eval_jaxpr/ppermute | solution.py:13
  298.3 3.1 collective-permute-done.5
  301.3 3.1 bitcast_add_fusion.2
  304.4 5.6 %collective-permute-start.3 = (f32[16,256]{1,0:T(8,128)S(1)}, f32[16,256]{1,0:T(8,128)S(1)}, u32[]{:S(2)}, u32[]{:S(2)}) collective-permute-start(f32[16,256]{1,0:T(8,128)S(1)} %get-tuple-element.334), channel_id=1, source_target_pairs={{0,127},{1,0},{2,1},{3,2},{4,3},{5,4},{6,5},{7,6},{8,7},{9,8},{10,... | collective-permute-start | bytes 49160 | tf_op jit(solution)/shard_map/while/body/eval_jaxpr/ppermute | solution.py:13
  310.2 4.4 fusion.104
  317.9 17.8 %collective-permute-done = bf16[256,2048]{0,1:T(8,128)(2,1)S(1)} collective-permute-done((bf16[256,2048]{0,1:T(8,128)(2,1)}, bf16[256,2048]{0,1:T(8,128)(2,1)S(1)}, u32[]{:S(2)}, u32[]{:S(2)}) %collective-permute-start) | collective-permute-done | bytes 1048608 | tf_op jit(solution)/shard_map/while/body/eval_jaxpr/ppermute | solution.py:13
  355.2 3.1 collective-permute-done.5
  358.3 3.1 bitcast_add_fusion.2
  361.4 5.6 %collective-permute-start.3 = (f32[16,256]{1,0:T(8,128)S(1)}, f32[16,256]{1,0:T(8,128)S(1)}, u32[]{:S(2)}, u32[]{:S(2)}) collective-permute-start(f32[16,256]{1,0:T(8,128)S(1)} %get-tuple-element.334), channel_id=1, source_target_pairs={{0,127},{1,0},{2,1},{3,2},{4,3},{5,4},{6,5},{7,6},{8,7},{9,8},{10,... | collective-permute-start | bytes 49160 | tf_op jit(solution)/shard_map/while/body/eval_jaxpr/ppermute | solution.py:13
  367.1 4.4 fusion.104
  374.9 17.8 %collective-permute-done = bf16[256,2048]{0,1:T(8,128)(2,1)S(1)} collective-permute-done((bf16[256,2048]{0,1:T(8,128)(2,1)}, bf16[256,2048]{0,1:T(8,128)(2,1)S(1)}, u32[]{:S(2)}, u32[]{:S(2)}) %collective-permute-start) | collective-permute-done | bytes 1048608 | tf_op jit(solution)/shard_map/while/body/eval_jaxpr/ppermute | solution.py:13
  412.2 3.1 collective-permute-done.5
  415.3 3.1 bitcast_add_fusion.2
  418.4 5.6 %collective-permute-start.3 = (f32[16,256]{1,0:T(8,128)S(1)}, f32[16,256]{1,0:T(8,128)S(1)}, u32[]{:S(2)}, u32[]{:S(2)}) collective-permute-start(f32[16,256]{1,0:T(8,128)S(1)} %get-tuple-element.334), channel_id=1, source_target_pairs={{0,127},{1,0},{2,1},{3,2},{4,3},{5,4},{6,5},{7,6},{8,7},{9,8},{10,... | collective-permute-start | bytes 49160 | tf_op jit(solution)/shard_map/while/body/eval_jaxpr/ppermute | solution.py:13
  424.1 4.4 fusion.104
  431.8 17.8 %collective-permute-done = bf16[256,2048]{0,1:T(8,128)(2,1)S(1)} collective-permute-done((bf16[256,2048]{0,1:T(8,128)(2,1)}, bf16[256,2048]{0,1:T(8,128)(2,1)S(1)}, u32[]{:S(2)}, u32[]{:S(2)}) %collective-permute-start) | collective-permute-done | bytes 1048608 | tf_op jit(solution)/shard_map/while/body/eval_jaxpr/ppermute | solution.py:13
  472.2 3.1 bitcast_add_fusion.2
  475.3 3.2 copy.50
  481.0 3.3 multiply_convert_fusion.2
  494.3 3.5 fusion.19
  499.2 4.6 copy.55
  503.8 4.7 copy.54
  508.5 19.6 %collective-permute-done.6 = f32[256,2048]{1,0:T(8,128)} collective-permute-done((f32[256,2048]{1,0:T(8,128)}, f32[256,2048]{1,0:T(8,128)}, u32[]{:S(2)}, u32[]{:S(2)}) %collective-permute-start.6) | collective-permute-done | bytes 2097184 | tf_op jit(solution)/shard_map/ppermute | solution.py:13
  (411 shorter events, 202.0 us)
Async XLA Ops:
  14.1 17.1 %collective-permute-start.4 = (s32[1,8]{1,0:T(1,128)S(1)}, s32[1,8]{1,0:T(1,128)S(1)}, u32[]{:S(2)}, u32[]{:S(2)}) collective-permute-start(s32[1,8]{1,0:T(1,128)S(1)} %get-tuple-element.335), channel_id=1, source_target_pairs={{0,127},{1,0},{2,1},{3,2},{4,3},{5,4},{6,5},{7,6},{8,7},{9,8},{10,... | collective-permute-start | bytes 104 | tf_op jit(solution)/shard_map/while/body/eval_jaxpr/ppermute | solution.py:13
  15.6 17.4 %collective-permute-start.3 = (f32[16,256]{1,0:T(8,128)S(1)}, f32[16,256]{1,0:T(8,128)S(1)}, u32[]{:S(2)}, u32[]{:S(2)}) collective-permute-start(f32[16,256]{1,0:T(8,128)S(1)} %get-tuple-element.334), channel_id=1, source_target_pairs={{0,127},{1,0},{2,1},{3,2},{4,3},{5,4},{6,5},{7,6},{8,7},{9,8},{10,... | collective-permute-start | bytes 49160 | tf_op jit(solution)/shard_map/while/body/eval_jaxpr/ppermute | solution.py:13
  23.8 9.3 %collective-permute-start.2 = (f32[16,256]{1,0:T(8,128)S(1)}, f32[16,256]{1,0:T(8,128)S(1)}, u32[]{:S(2)}, u32[]{:S(2)}) collective-permute-start(f32[16,256]{1,0:T(8,128)S(1)} %get-tuple-element.333), channel_id=1, source_target_pairs={{0,127},{1,0},{2,1},{3,2},{4,3},{5,4},{6,5},{7,6},{8,7},{9,8},{10,... | collective-permute-start | bytes 49160 | tf_op jit(solution)/shard_map/while/body/eval_jaxpr/ppermute | solution.py:13
  24.5 27.6 %collective-permute-start.1 = (bf16[256,2048]{0,1:T(8,128)(2,1)}, bf16[256,2048]{0,1:T(8,128)(2,1)S(1)}, u32[]{:S(2)}, u32[]{:S(2)}) collective-permute-start(bf16[256,2048]{0,1:T(8,128)(2,1)} %get-tuple-element.332), channel_id=1, source_target_pairs={{0,127},{1,0},{2,1},{3,2},{4,3},{5,4},{6,5},{7,6},{8,7},{9,8},{10,... | collective-permute-start | bytes 3145736 | tf_op jit(solution)/shard_map/while/body/eval_jaxpr/ppermute | solution.py:13
  24.7 25.5 %collective-permute-start = (bf16[256,2048]{0,1:T(8,128)(2,1)}, bf16[256,2048]{0,1:T(8,128)(2,1)S(1)}, u32[]{:S(2)}, u32[]{:S(2)}) collective-permute-start(bf16[256,2048]{0,1:T(8,128)(2,1)} %get-tuple-element.331), channel_id=1, source_target_pairs={{0,127},{1,0},{2,1},{3,2},{4,3},{5,4},{6,5},{7,6},{8,7},{9,8},{10,... | collective-permute-start | bytes 3145736 | tf_op jit(solution)/shard_map/while/body/eval_jaxpr/ppermute | solution.py:13
  31.2 41.6 %collective-permute-start.5 = (f32[256,2048]{0,1:T(8,128)}, f32[256,2048]{0,1:T(8,128)}, u32[]{:S(2)}, u32[]{:S(2)}) collective-permute-start(f32[256,2048]{0,1:T(8,128)} %broadcast_select_fusion.2), channel_id=1, source_target_pairs={{0,127},{1,0},{2,1},{3,2},{4,3},{5,4},{6,5},{7,6},{8,7},{9,8},{10,... | collective-permute-start | bytes 6291464 | tf_op jit(solution)/shard_map/while/body/eval_jaxpr/ppermute | solution.py:13
  75.9 12.3 %collective-permute-start.4 = (s32[1,8]{1,0:T(1,128)S(1)}, s32[1,8]{1,0:T(1,128)S(1)}, u32[]{:S(2)}, u32[]{:S(2)}) collective-permute-start(s32[1,8]{1,0:T(1,128)S(1)} %get-tuple-element.335), channel_id=1, source_target_pairs={{0,127},{1,0},{2,1},{3,2},{4,3},{5,4},{6,5},{7,6},{8,7},{9,8},{10,... | collective-permute-start | bytes 104 | tf_op jit(solution)/shard_map/while/body/eval_jaxpr/ppermute | solution.py:13
  75.9 14.2 %collective-permute-start.3 = (f32[16,256]{1,0:T(8,128)S(1)}, f32[16,256]{1,0:T(8,128)S(1)}, u32[]{:S(2)}, u32[]{:S(2)}) collective-permute-start(f32[16,256]{1,0:T(8,128)S(1)} %get-tuple-element.334), channel_id=1, source_target_pairs={{0,127},{1,0},{2,1},{3,2},{4,3},{5,4},{6,5},{7,6},{8,7},{9,8},{10,... | collective-permute-start | bytes 49160 | tf_op jit(solution)/shard_map/while/body/eval_jaxpr/ppermute | solution.py:13
  82.2 7.9 %collective-permute-start.2 = (f32[16,256]{1,0:T(8,128)S(1)}, f32[16,256]{1,0:T(8,128)S(1)}, u32[]{:S(2)}, u32[]{:S(2)}) collective-permute-start(f32[16,256]{1,0:T(8,128)S(1)} %get-tuple-element.333), channel_id=1, source_target_pairs={{0,127},{1,0},{2,1},{3,2},{4,3},{5,4},{6,5},{7,6},{8,7},{9,8},{10,... | collective-permute-start | bytes 49160 | tf_op jit(solution)/shard_map/while/body/eval_jaxpr/ppermute | solution.py:13
  82.2 27.7 %collective-permute-start.1 = (bf16[256,2048]{0,1:T(8,128)(2,1)}, bf16[256,2048]{0,1:T(8,128)(2,1)S(1)}, u32[]{:S(2)}, u32[]{:S(2)}) collective-permute-start(bf16[256,2048]{0,1:T(8,128)(2,1)} %get-tuple-element.332), channel_id=1, source_target_pairs={{0,127},{1,0},{2,1},{3,2},{4,3},{5,4},{6,5},{7,6},{8,7},{9,8},{10,... | collective-permute-start | bytes 3145736 | tf_op jit(solution)/shard_map/while/body/eval_jaxpr/ppermute | solution.py:13
  82.2 25.6 %collective-permute-start = (bf16[256,2048]{0,1:T(8,128)(2,1)}, bf16[256,2048]{0,1:T(8,128)(2,1)S(1)}, u32[]{:S(2)}, u32[]{:S(2)}) collective-permute-start(bf16[256,2048]{0,1:T(8,128)(2,1)} %get-tuple-element.331), channel_id=1, source_target_pairs={{0,127},{1,0},{2,1},{3,2},{4,3},{5,4},{6,5},{7,6},{8,7},{9,8},{10,... | collective-permute-start | bytes 3145736 | tf_op jit(solution)/shard_map/while/body/eval_jaxpr/ppermute | solution.py:13
  88.1 42.3 %collective-permute-start.5 = (f32[256,2048]{0,1:T(8,128)}, f32[256,2048]{0,1:T(8,128)}, u32[]{:S(2)}, u32[]{:S(2)}) collective-permute-start(f32[256,2048]{0,1:T(8,128)} %broadcast_select_fusion.2), channel_id=1, source_target_pairs={{0,127},{1,0},{2,1},{3,2},{4,3},{5,4},{6,5},{7,6},{8,7},{9,8},{10,... | collective-permute-start | bytes 6291464 | tf_op jit(solution)/shard_map/while/body/eval_jaxpr/ppermute | solution.py:13
  133.6 11.5 %collective-permute-start.4 = (s32[1,8]{1,0:T(1,128)S(1)}, s32[1,8]{1,0:T(1,128)S(1)}, u32[]{:S(2)}, u32[]{:S(2)}) collective-permute-start(s32[1,8]{1,0:T(1,128)S(1)} %get-tuple-element.335), channel_id=1, source_target_pairs={{0,127},{1,0},{2,1},{3,2},{4,3},{5,4},{6,5},{7,6},{8,7},{9,8},{10,... | collective-permute-start | bytes 104 | tf_op jit(solution)/shard_map/while/body/eval_jaxpr/ppermute | solution.py:13
  133.6 13.4 %collective-permute-start.3 = (f32[16,256]{1,0:T(8,128)S(1)}, f32[16,256]{1,0:T(8,128)S(1)}, u32[]{:S(2)}, u32[]{:S(2)}) collective-permute-start(f32[16,256]{1,0:T(8,128)S(1)} %get-tuple-element.334), channel_id=1, source_target_pairs={{0,127},{1,0},{2,1},{3,2},{4,3},{5,4},{6,5},{7,6},{8,7},{9,8},{10,... | collective-permute-start | bytes 49160 | tf_op jit(solution)/shard_map/while/body/eval_jaxpr/ppermute | solution.py:13
  139.1 7.9 %collective-permute-start.2 = (f32[16,256]{1,0:T(8,128)S(1)}, f32[16,256]{1,0:T(8,128)S(1)}, u32[]{:S(2)}, u32[]{:S(2)}) collective-permute-start(f32[16,256]{1,0:T(8,128)S(1)} %get-tuple-element.333), channel_id=1, source_target_pairs={{0,127},{1,0},{2,1},{3,2},{4,3},{5,4},{6,5},{7,6},{8,7},{9,8},{10,... | collective-permute-start | bytes 49160 | tf_op jit(solution)/shard_map/while/body/eval_jaxpr/ppermute | solution.py:13
  139.2 27.7 %collective-permute-start.1 = (bf16[256,2048]{0,1:T(8,128)(2,1)}, bf16[256,2048]{0,1:T(8,128)(2,1)S(1)}, u32[]{:S(2)}, u32[]{:S(2)}) collective-permute-start(bf16[256,2048]{0,1:T(8,128)(2,1)} %get-tuple-element.332), channel_id=1, source_target_pairs={{0,127},{1,0},{2,1},{3,2},{4,3},{5,4},{6,5},{7,6},{8,7},{9,8},{10,... | collective-permute-start | bytes 3145736 | tf_op jit(solution)/shard_map/while/body/eval_jaxpr/ppermute | solution.py:13
  139.2 25.6 %collective-permute-start = (bf16[256,2048]{0,1:T(8,128)(2,1)}, bf16[256,2048]{0,1:T(8,128)(2,1)S(1)}, u32[]{:S(2)}, u32[]{:S(2)}) collective-permute-start(bf16[256,2048]{0,1:T(8,128)(2,1)} %get-tuple-element.331), channel_id=1, source_target_pairs={{0,127},{1,0},{2,1},{3,2},{4,3},{5,4},{6,5},{7,6},{8,7},{9,8},{10,... | collective-permute-start | bytes 3145736 | tf_op jit(solution)/shard_map/while/body/eval_jaxpr/ppermute | solution.py:13
  145.1 42.3 %collective-permute-start.5 = (f32[256,2048]{0,1:T(8,128)}, f32[256,2048]{0,1:T(8,128)}, u32[]{:S(2)}, u32[]{:S(2)}) collective-permute-start(f32[256,2048]{0,1:T(8,128)} %broadcast_select_fusion.2), channel_id=1, source_target_pairs={{0,127},{1,0},{2,1},{3,2},{4,3},{5,4},{6,5},{7,6},{8,7},{9,8},{10,... | collective-permute-start | bytes 6291464 | tf_op jit(solution)/shard_map/while/body/eval_jaxpr/ppermute | solution.py:13
  190.5 11.5 %collective-permute-start.4 = (s32[1,8]{1,0:T(1,128)S(1)}, s32[1,8]{1,0:T(1,128)S(1)}, u32[]{:S(2)}, u32[]{:S(2)}) collective-permute-start(s32[1,8]{1,0:T(1,128)S(1)} %get-tuple-element.335), channel_id=1, source_target_pairs={{0,127},{1,0},{2,1},{3,2},{4,3},{5,4},{6,5},{7,6},{8,7},{9,8},{10,... | collective-permute-start | bytes 104 | tf_op jit(solution)/shard_map/while/body/eval_jaxpr/ppermute | solution.py:13
  190.5 13.4 %collective-permute-start.3 = (f32[16,256]{1,0:T(8,128)S(1)}, f32[16,256]{1,0:T(8,128)S(1)}, u32[]{:S(2)}, u32[]{:S(2)}) collective-permute-start(f32[16,256]{1,0:T(8,128)S(1)} %get-tuple-element.334), channel_id=1, source_target_pairs={{0,127},{1,0},{2,1},{3,2},{4,3},{5,4},{6,5},{7,6},{8,7},{9,8},{10,... | collective-permute-start | bytes 49160 | tf_op jit(solution)/shard_map/while/body/eval_jaxpr/ppermute | solution.py:13
  196.1 7.9 %collective-permute-start.2 = (f32[16,256]{1,0:T(8,128)S(1)}, f32[16,256]{1,0:T(8,128)S(1)}, u32[]{:S(2)}, u32[]{:S(2)}) collective-permute-start(f32[16,256]{1,0:T(8,128)S(1)} %get-tuple-element.333), channel_id=1, source_target_pairs={{0,127},{1,0},{2,1},{3,2},{4,3},{5,4},{6,5},{7,6},{8,7},{9,8},{10,... | collective-permute-start | bytes 49160 | tf_op jit(solution)/shard_map/while/body/eval_jaxpr/ppermute | solution.py:13
  196.1 27.7 %collective-permute-start.1 = (bf16[256,2048]{0,1:T(8,128)(2,1)}, bf16[256,2048]{0,1:T(8,128)(2,1)S(1)}, u32[]{:S(2)}, u32[]{:S(2)}) collective-permute-start(bf16[256,2048]{0,1:T(8,128)(2,1)} %get-tuple-element.332), channel_id=1, source_target_pairs={{0,127},{1,0},{2,1},{3,2},{4,3},{5,4},{6,5},{7,6},{8,7},{9,8},{10,... | collective-permute-start | bytes 3145736 | tf_op jit(solution)/shard_map/while/body/eval_jaxpr/ppermute | solution.py:13
  196.2 25.6 %collective-permute-start = (bf16[256,2048]{0,1:T(8,128)(2,1)}, bf16[256,2048]{0,1:T(8,128)(2,1)S(1)}, u32[]{:S(2)}, u32[]{:S(2)}) collective-permute-start(bf16[256,2048]{0,1:T(8,128)(2,1)} %get-tuple-element.331), channel_id=1, source_target_pairs={{0,127},{1,0},{2,1},{3,2},{4,3},{5,4},{6,5},{7,6},{8,7},{9,8},{10,... | collective-permute-start | bytes 3145736 | tf_op jit(solution)/shard_map/while/body/eval_jaxpr/ppermute | solution.py:13
  202.1 42.3 %collective-permute-start.5 = (f32[256,2048]{0,1:T(8,128)}, f32[256,2048]{0,1:T(8,128)}, u32[]{:S(2)}, u32[]{:S(2)}) collective-permute-start(f32[256,2048]{0,1:T(8,128)} %broadcast_select_fusion.2), channel_id=1, source_target_pairs={{0,127},{1,0},{2,1},{3,2},{4,3},{5,4},{6,5},{7,6},{8,7},{9,8},{10,... | collective-permute-start | bytes 6291464 | tf_op jit(solution)/shard_map/while/body/eval_jaxpr/ppermute | solution.py:13
  247.5 11.5 %collective-permute-start.4 = (s32[1,8]{1,0:T(1,128)S(1)}, s32[1,8]{1,0:T(1,128)S(1)}, u32[]{:S(2)}, u32[]{:S(2)}) collective-permute-start(s32[1,8]{1,0:T(1,128)S(1)} %get-tuple-element.335), channel_id=1, source_target_pairs={{0,127},{1,0},{2,1},{3,2},{4,3},{5,4},{6,5},{7,6},{8,7},{9,8},{10,... | collective-permute-start | bytes 104 | tf_op jit(solution)/shard_map/while/body/eval_jaxpr/ppermute | solution.py:13
  247.5 13.4 %collective-permute-start.3 = (f32[16,256]{1,0:T(8,128)S(1)}, f32[16,256]{1,0:T(8,128)S(1)}, u32[]{:S(2)}, u32[]{:S(2)}) collective-permute-start(f32[16,256]{1,0:T(8,128)S(1)} %get-tuple-element.334), channel_id=1, source_target_pairs={{0,127},{1,0},{2,1},{3,2},{4,3},{5,4},{6,5},{7,6},{8,7},{9,8},{10,... | collective-permute-start | bytes 49160 | tf_op jit(solution)/shard_map/while/body/eval_jaxpr/ppermute | solution.py:13
  253.0 7.9 %collective-permute-start.2 = (f32[16,256]{1,0:T(8,128)S(1)}, f32[16,256]{1,0:T(8,128)S(1)}, u32[]{:S(2)}, u32[]{:S(2)}) collective-permute-start(f32[16,256]{1,0:T(8,128)S(1)} %get-tuple-element.333), channel_id=1, source_target_pairs={{0,127},{1,0},{2,1},{3,2},{4,3},{5,4},{6,5},{7,6},{8,7},{9,8},{10,... | collective-permute-start | bytes 49160 | tf_op jit(solution)/shard_map/while/body/eval_jaxpr/ppermute | solution.py:13
  253.1 27.7 %collective-permute-start.1 = (bf16[256,2048]{0,1:T(8,128)(2,1)}, bf16[256,2048]{0,1:T(8,128)(2,1)S(1)}, u32[]{:S(2)}, u32[]{:S(2)}) collective-permute-start(bf16[256,2048]{0,1:T(8,128)(2,1)} %get-tuple-element.332), channel_id=1, source_target_pairs={{0,127},{1,0},{2,1},{3,2},{4,3},{5,4},{6,5},{7,6},{8,7},{9,8},{10,... | collective-permute-start | bytes 3145736 | tf_op jit(solution)/shard_map/while/body/eval_jaxpr/ppermute | solution.py:13
  253.1 25.6 %collective-permute-start = (bf16[256,2048]{0,1:T(8,128)(2,1)}, bf16[256,2048]{0,1:T(8,128)(2,1)S(1)}, u32[]{:S(2)}, u32[]{:S(2)}) collective-permute-start(bf16[256,2048]{0,1:T(8,128)(2,1)} %get-tuple-element.331), channel_id=1, source_target_pairs={{0,127},{1,0},{2,1},{3,2},{4,3},{5,4},{6,5},{7,6},{8,7},{9,8},{10,... | collective-permute-start | bytes 3145736 | tf_op jit(solution)/shard_map/while/body/eval_jaxpr/ppermute | solution.py:13
  259.0 42.3 %collective-permute-start.5 = (f32[256,2048]{0,1:T(8,128)}, f32[256,2048]{0,1:T(8,128)}, u32[]{:S(2)}, u32[]{:S(2)}) collective-permute-start(f32[256,2048]{0,1:T(8,128)} %broadcast_select_fusion.2), channel_id=1, source_target_pairs={{0,127},{1,0},{2,1},{3,2},{4,3},{5,4},{6,5},{7,6},{8,7},{9,8},{10,... | collective-permute-start | bytes 6291464 | tf_op jit(solution)/shard_map/while/body/eval_jaxpr/ppermute | solution.py:13
  304.4 11.5 %collective-permute-start.4 = (s32[1,8]{1,0:T(1,128)S(1)}, s32[1,8]{1,0:T(1,128)S(1)}, u32[]{:S(2)}, u32[]{:S(2)}) collective-permute-start(s32[1,8]{1,0:T(1,128)S(1)} %get-tuple-element.335), channel_id=1, source_target_pairs={{0,127},{1,0},{2,1},{3,2},{4,3},{5,4},{6,5},{7,6},{8,7},{9,8},{10,... | collective-permute-start | bytes 104 | tf_op jit(solution)/shard_map/while/body/eval_jaxpr/ppermute | solution.py:13
  304.4 13.4 %collective-permute-start.3 = (f32[16,256]{1,0:T(8,128)S(1)}, f32[16,256]{1,0:T(8,128)S(1)}, u32[]{:S(2)}, u32[]{:S(2)}) collective-permute-start(f32[16,256]{1,0:T(8,128)S(1)} %get-tuple-element.334), channel_id=1, source_target_pairs={{0,127},{1,0},{2,1},{3,2},{4,3},{5,4},{6,5},{7,6},{8,7},{9,8},{10,... | collective-permute-start | bytes 49160 | tf_op jit(solution)/shard_map/while/body/eval_jaxpr/ppermute | solution.py:13
  310.0 7.9 %collective-permute-start.2 = (f32[16,256]{1,0:T(8,128)S(1)}, f32[16,256]{1,0:T(8,128)S(1)}, u32[]{:S(2)}, u32[]{:S(2)}) collective-permute-start(f32[16,256]{1,0:T(8,128)S(1)} %get-tuple-element.333), channel_id=1, source_target_pairs={{0,127},{1,0},{2,1},{3,2},{4,3},{5,4},{6,5},{7,6},{8,7},{9,8},{10,... | collective-permute-start | bytes 49160 | tf_op jit(solution)/shard_map/while/body/eval_jaxpr/ppermute | solution.py:13
  310.0 27.7 %collective-permute-start.1 = (bf16[256,2048]{0,1:T(8,128)(2,1)}, bf16[256,2048]{0,1:T(8,128)(2,1)S(1)}, u32[]{:S(2)}, u32[]{:S(2)}) collective-permute-start(bf16[256,2048]{0,1:T(8,128)(2,1)} %get-tuple-element.332), channel_id=1, source_target_pairs={{0,127},{1,0},{2,1},{3,2},{4,3},{5,4},{6,5},{7,6},{8,7},{9,8},{10,... | collective-permute-start | bytes 3145736 | tf_op jit(solution)/shard_map/while/body/eval_jaxpr/ppermute | solution.py:13
  310.1 25.6 %collective-permute-start = (bf16[256,2048]{0,1:T(8,128)(2,1)}, bf16[256,2048]{0,1:T(8,128)(2,1)S(1)}, u32[]{:S(2)}, u32[]{:S(2)}) collective-permute-start(bf16[256,2048]{0,1:T(8,128)(2,1)} %get-tuple-element.331), channel_id=1, source_target_pairs={{0,127},{1,0},{2,1},{3,2},{4,3},{5,4},{6,5},{7,6},{8,7},{9,8},{10,... | collective-permute-start | bytes 3145736 | tf_op jit(solution)/shard_map/while/body/eval_jaxpr/ppermute | solution.py:13
  316.0 42.3 %collective-permute-start.5 = (f32[256,2048]{0,1:T(8,128)}, f32[256,2048]{0,1:T(8,128)}, u32[]{:S(2)}, u32[]{:S(2)}) collective-permute-start(f32[256,2048]{0,1:T(8,128)} %broadcast_select_fusion.2), channel_id=1, source_target_pairs={{0,127},{1,0},{2,1},{3,2},{4,3},{5,4},{6,5},{7,6},{8,7},{9,8},{10,... | collective-permute-start | bytes 6291464 | tf_op jit(solution)/shard_map/while/body/eval_jaxpr/ppermute | solution.py:13
  361.4 11.5 %collective-permute-start.4 = (s32[1,8]{1,0:T(1,128)S(1)}, s32[1,8]{1,0:T(1,128)S(1)}, u32[]{:S(2)}, u32[]{:S(2)}) collective-permute-start(s32[1,8]{1,0:T(1,128)S(1)} %get-tuple-element.335), channel_id=1, source_target_pairs={{0,127},{1,0},{2,1},{3,2},{4,3},{5,4},{6,5},{7,6},{8,7},{9,8},{10,... | collective-permute-start | bytes 104 | tf_op jit(solution)/shard_map/while/body/eval_jaxpr/ppermute | solution.py:13
  361.4 13.4 %collective-permute-start.3 = (f32[16,256]{1,0:T(8,128)S(1)}, f32[16,256]{1,0:T(8,128)S(1)}, u32[]{:S(2)}, u32[]{:S(2)}) collective-permute-start(f32[16,256]{1,0:T(8,128)S(1)} %get-tuple-element.334), channel_id=1, source_target_pairs={{0,127},{1,0},{2,1},{3,2},{4,3},{5,4},{6,5},{7,6},{8,7},{9,8},{10,... | collective-permute-start | bytes 49160 | tf_op jit(solution)/shard_map/while/body/eval_jaxpr/ppermute | solution.py:13
  367.0 7.9 %collective-permute-start.2 = (f32[16,256]{1,0:T(8,128)S(1)}, f32[16,256]{1,0:T(8,128)S(1)}, u32[]{:S(2)}, u32[]{:S(2)}) collective-permute-start(f32[16,256]{1,0:T(8,128)S(1)} %get-tuple-element.333), channel_id=1, source_target_pairs={{0,127},{1,0},{2,1},{3,2},{4,3},{5,4},{6,5},{7,6},{8,7},{9,8},{10,... | collective-permute-start | bytes 49160 | tf_op jit(solution)/shard_map/while/body/eval_jaxpr/ppermute | solution.py:13
  367.0 27.7 %collective-permute-start.1 = (bf16[256,2048]{0,1:T(8,128)(2,1)}, bf16[256,2048]{0,1:T(8,128)(2,1)S(1)}, u32[]{:S(2)}, u32[]{:S(2)}) collective-permute-start(bf16[256,2048]{0,1:T(8,128)(2,1)} %get-tuple-element.332), channel_id=1, source_target_pairs={{0,127},{1,0},{2,1},{3,2},{4,3},{5,4},{6,5},{7,6},{8,7},{9,8},{10,... | collective-permute-start | bytes 3145736 | tf_op jit(solution)/shard_map/while/body/eval_jaxpr/ppermute | solution.py:13
  367.0 25.6 %collective-permute-start = (bf16[256,2048]{0,1:T(8,128)(2,1)}, bf16[256,2048]{0,1:T(8,128)(2,1)S(1)}, u32[]{:S(2)}, u32[]{:S(2)}) collective-permute-start(bf16[256,2048]{0,1:T(8,128)(2,1)} %get-tuple-element.331), channel_id=1, source_target_pairs={{0,127},{1,0},{2,1},{3,2},{4,3},{5,4},{6,5},{7,6},{8,7},{9,8},{10,... | collective-permute-start | bytes 3145736 | tf_op jit(solution)/shard_map/while/body/eval_jaxpr/ppermute | solution.py:13
  372.9 42.3 %collective-permute-start.5 = (f32[256,2048]{0,1:T(8,128)}, f32[256,2048]{0,1:T(8,128)}, u32[]{:S(2)}, u32[]{:S(2)}) collective-permute-start(f32[256,2048]{0,1:T(8,128)} %broadcast_select_fusion.2), channel_id=1, source_target_pairs={{0,127},{1,0},{2,1},{3,2},{4,3},{5,4},{6,5},{7,6},{8,7},{9,8},{10,... | collective-permute-start | bytes 6291464 | tf_op jit(solution)/shard_map/while/body/eval_jaxpr/ppermute | solution.py:13
  418.4 11.5 %collective-permute-start.4 = (s32[1,8]{1,0:T(1,128)S(1)}, s32[1,8]{1,0:T(1,128)S(1)}, u32[]{:S(2)}, u32[]{:S(2)}) collective-permute-start(s32[1,8]{1,0:T(1,128)S(1)} %get-tuple-element.335), channel_id=1, source_target_pairs={{0,127},{1,0},{2,1},{3,2},{4,3},{5,4},{6,5},{7,6},{8,7},{9,8},{10,... | collective-permute-start | bytes 104 | tf_op jit(solution)/shard_map/while/body/eval_jaxpr/ppermute | solution.py:13
  418.4 13.4 %collective-permute-start.3 = (f32[16,256]{1,0:T(8,128)S(1)}, f32[16,256]{1,0:T(8,128)S(1)}, u32[]{:S(2)}, u32[]{:S(2)}) collective-permute-start(f32[16,256]{1,0:T(8,128)S(1)} %get-tuple-element.334), channel_id=1, source_target_pairs={{0,127},{1,0},{2,1},{3,2},{4,3},{5,4},{6,5},{7,6},{8,7},{9,8},{10,... | collective-permute-start | bytes 49160 | tf_op jit(solution)/shard_map/while/body/eval_jaxpr/ppermute | solution.py:13
  424.0 27.7 %collective-permute-start.1 = (bf16[256,2048]{0,1:T(8,128)(2,1)}, bf16[256,2048]{0,1:T(8,128)(2,1)S(1)}, u32[]{:S(2)}, u32[]{:S(2)}) collective-permute-start(bf16[256,2048]{0,1:T(8,128)(2,1)} %get-tuple-element.332), channel_id=1, source_target_pairs={{0,127},{1,0},{2,1},{3,2},{4,3},{5,4},{6,5},{7,6},{8,7},{9,8},{10,... | collective-permute-start | bytes 3145736 | tf_op jit(solution)/shard_map/while/body/eval_jaxpr/ppermute | solution.py:13
  424.0 25.6 %collective-permute-start = (bf16[256,2048]{0,1:T(8,128)(2,1)}, bf16[256,2048]{0,1:T(8,128)(2,1)S(1)}, u32[]{:S(2)}, u32[]{:S(2)}) collective-permute-start(bf16[256,2048]{0,1:T(8,128)(2,1)} %get-tuple-element.331), channel_id=1, source_target_pairs={{0,127},{1,0},{2,1},{3,2},{4,3},{5,4},{6,5},{7,6},{8,7},{9,8},{10,... | collective-permute-start | bytes 3145736 | tf_op jit(solution)/shard_map/while/body/eval_jaxpr/ppermute | solution.py:13
  429.9 42.3 %collective-permute-start.5 = (f32[256,2048]{0,1:T(8,128)}, f32[256,2048]{0,1:T(8,128)}, u32[]{:S(2)}, u32[]{:S(2)}) collective-permute-start(f32[256,2048]{0,1:T(8,128)} %broadcast_select_fusion.2), channel_id=1, source_target_pairs={{0,127},{1,0},{2,1},{3,2},{4,3},{5,4},{6,5},{7,6},{8,7},{9,8},{10,... | collective-permute-start | bytes 6291464 | tf_op jit(solution)/shard_map/while/body/eval_jaxpr/ppermute | solution.py:13
  478.5 49.7 %collective-permute-start.6 = (f32[256,2048]{1,0:T(8,128)}, f32[256,2048]{1,0:T(8,128)}, u32[]{:S(2)}, u32[]{:S(2)}) collective-permute-start(f32[256,2048]{1,0:T(8,128)} %copy.50), channel_id=1, source_target_pairs={{0,8},{1,9},{2,10},{3,11},{4,12},{5,13},{6,14},{7,15},{8,16},{9,17... | collective-permute-start | bytes 6291464 | tf_op jit(solution)/shard_map/ppermute | solution.py:13
  (86 other events, 903.5 us)
where the time goes:
time: 533 us; the launch traced here: 531 us
  waiting for transfers between devices  186 us (35%)
  matrix products  116 us (22%)
  local copies, waits for them, and re-layouts  99.9 us (19%)
  other arithmetic  64.6 us (12%)
  starting transfers between devices  52.6 us (10%)
  loops' own time  10.8 us (2%)
    ppermute x49, waiting for transfers between devices, from_behind(): return lax.ppermute(value, axis, pairs)  186 us
    ppermute x49, starting transfers between devices, from_behind(): return lax.ppermute(value, axis, pairs)  52.6 us
    dot_general x17, matrix products, pair_grads(): jnp.einsum('qhd,khd->hqk', o_heads, v_heads, preferred_element_type=jnp.f...  36.2 us
    slice x8, local copies, waits for them, and re-layouts, visit(): values = v_clean[slot * rows:(slot + 1) * rows]  34.9 us
    dot_general x17, matrix products, pair_grads(): jnp.einsum('hqk,qhd->khd', probs_low, o_heads, preferred_element_type=jnp...  32.4 us
    while x184, local copies, waits for them, and re-layouts  30.8 us
    add x8, other arithmetic, cycle_step(): acc_q + part_q  24.9 us
    dot_general x17, matrix products, pair_grads(): jnp.einsum('qhd,khd->hqk', q_heads, k_heads, preferred_element_type=jnp.f...  22.6 us
  transfers between devices with their start and end apart: 49, of which 17 were waited for; matrix products, arithmetic and copies ran while one was open for 42% of the time, Pallas kernels for 0%

commit v1 on v0

v1 whole, which is shorter than its diff:
```python
import functools

import jax
import jax.numpy as jnp
from jax import lax
from jax.experimental import pallas as pl
from jax.experimental.pallas import tpu as pltpu
from jax.sharding import PartitionSpec as P

F32 = jnp.float32
BF16 = jnp.bfloat16
HD = 128
BLK = 256
CLEAN = 512
KEYS = 1024
RING = 4
SCALE = HD**-0.5
LOG2E = 1.4426950408889634
FAR_OFF = 1e30
STAT = 24

OWN, SAME, UP, DOWN, FAR = range(5)


def dot_nt(a, b):
    return lax.dot_general(a, b, (((1,), (1,)), ((), ())), preferred_element_type=F32)


def dot_nn(a, b):
    return lax.dot_general(a, b, (((1,), (0,)), ((), ())), preferred_element_type=F32)


def dot_tn(a, b):
    return lax.dot_general(a, b, (((0,), (0,)), ((), ())), preferred_element_type=F32)


def kernel(
    rows, nh,
    q, do, kn, vn, kc, vc, lse, delta, listed,
    dq, dkn, dvn, dkc, dvc,
    qd, kv, ms, st, mine, oq, near_p, same_p, ak, av, dkv, fs, fr, ns, nr, xs, xr, gs, gr, on, dqs,
    s_mine, s_loc, s_d2d, r_d2d, s_sd, r_sd,
    s_x, r_x, s_dn, r_dn, s_up, r_up, s_rd, s_ru, r_far,
    s_f, r_f, s_n, r_n, s_b, r_b, s_g, r_g, s_ol, s_or, r_or, s_on, s_dq,
):
    me = lax.axis_index("ctx")
    p = lax.rem(me, 2)
    j = lax.rem(me // 2, RING)
    r = me // (2 * RING)

    def dev(row, col, core):
        return row * (2 * RING) + col * 2 + core

    j_up, j_dn = lax.rem(j + 1, RING), lax.rem(j + RING - 1, RING)
    r_nx, r_pv = lax.rem(r + 1, rows), lax.rem(r + rows - 1, rows)
    sib = dev(r, j, 1 - p)
    up, dn, prev = dev(r, j_up, p), dev(r, j_dn, p), dev(r_pv, j, p)
    middle = jnp.logical_and(j >= 1, j <= 2)
    far_dir = jnp.where(j <= 1, 0, 1)
    far_to = jnp.where(j <= 1, up, dn)

    def remote(src, dst, ss, rs, to):
        return pltpu.make_async_remote_copy(
            src_ref=src, dst_ref=dst, send_sem=ss, recv_sem=rs,
            device_id=(to,), device_id_type=pl.DeviceIdType.MESH,
        )

    def cols(plane, g):
        return pl.ds(pl.multiple_of((plane * nh + g) * HD, HD), HD)

    my_rows = pl.ds(pl.multiple_of(p * CLEAN, CLEAN), CLEAN)
    other_rows = pl.ds(pl.multiple_of((1 - p) * CLEAN, CLEAN), CLEAN)

    def swap_places(g):
        return (
            (q, qd.at[OWN, g, p, 0]),
            (do, qd.at[OWN, g, p, 1]),
            (kc, kv.at[g, 0, my_rows]),
            (vc, kv.at[g, 1, my_rows]),
        )

    def swap_recv_places(g):
        return (
            (q, qd.at[OWN, g, 1 - p, 0]),
            (do, qd.at[OWN, g, 1 - p, 1]),
            (kc, kv.at[g, 0, other_rows]),
            (vc, kv.at[g, 1, other_rows]),
        )

    def swap_start(g):
        for n, (src, dst) in enumerate(swap_places(g)):
            remote(src.at[:, cols(1 - p, g)], dst, s_d2d.at[n, g], r_d2d.at[n, g], sib).start()
            pltpu.make_async_copy(src.at[:, cols(p, g)], dst, s_loc.at[n, g]).start()

    def swap_wait(g):
        for n, (src, dst) in enumerate(swap_places(g)):
            pltpu.make_async_copy(src.at[:, cols(p, g)], dst, s_loc.at[n, g]).wait()
        for n, (src, dst) in enumerate(swap_recv_places(g)):
            remote(src.at[:, cols(1 - p, g)], dst, s_d2d.at[n, g], r_d2d.at[n, g], sib).wait_recv()

    def swap_done(g):
        for n, (src, dst) in enumerate(swap_places(g)):
            remote(src.at[:, cols(1 - p, g)], dst, s_d2d.at[n, g], r_d2d.at[n, g], sib).wait_send()

    class Load:
        def __init__(self, ref, i, stats):
            self.i = i
            self.at = (lambda s: ref.at[s]) if stats else (lambda s: ref.at[s, i])
            self.blk = (lambda s, b: ref.at[s, b]) if stats else (lambda s, b: ref.at[s, i, b])

        def to_prev(self):
            return remote(self.at(OWN), self.at(SAME), s_x.at[self.i], r_x.at[self.i], prev)

        def down(self, slot):
            return remote(self.at(slot), self.at(UP), s_dn.at[self.i], r_dn.at[self.i], dn)

        def up(self, slot):
            return remote(self.at(slot), self.at(DOWN), s_up.at[self.i], r_up.at[self.i], up)

        def relay_down(self, b):
            return remote(
                self.blk(UP, b), self.blk(FAR, b), s_rd.at[b, self.i], r_far.at[b, self.i], dn
            )

        def relay_up(self, b):
            return remote(
                self.blk(DOWN, b), self.blk(FAR, b), s_ru.at[b, self.i], r_far.at[b, self.i], up
            )

        def send_own(self):
            self.to_prev().start()
            pl.when(j > 0)(lambda: self.down(OWN).start())
            pl.when(j == RING - 1)(lambda: self.up(OWN).start())

        def send_same(self):
            self.to_prev().wait_recv()
            pl.when(j == 0)(lambda: self.down(SAME).start())
            pl.when(j < RING - 1)(lambda: self.up(SAME).start())

        def relay(self):
            self.down(OWN).wait_recv()
            pl.when(j >= 1)(lambda: self.relay_down(0).start())
            pl.when(j == 1)(lambda: self.relay_down(1).start())
            self.up(OWN).wait_recv()
            pl.when(j <= 2)(lambda: self.relay_up(1).start())
            pl.when(j == 2)(lambda: self.relay_up(0).start())

        def far_wait(self):
            self.relay_down(0).wait_recv()
            self.relay_up(1).wait_recv()

        def done(self):
            self.to_prev().wait_send()
            self.down(OWN).wait_send()
            self.up(OWN).wait_send()
            pl.when(j >= 1)(lambda: self.relay_down(0).wait_send())
            pl.when(j == 1)(lambda: self.relay_down(1).wait_send())
            pl.when(j <= 2)(lambda: self.relay_up(1).wait_send())
            pl.when(j == 2)(lambda: self.relay_up(0).wait_send())

    def load(g):
        return Load(qd, g, False)

    stats = Load(st, nh, True)

    def far_copy(g):
        return remote(fs.at[g], fr.at[far_dir, g], s_f.at[g], r_f.at[far_dir, g], far_to)

    def far_recv(d, g):
        return remote(fs.at[g], fr.at[d, g], s_f.at[g], r_f.at[d, g], far_to)

    def near_copy(d, b, g):
        col = j_up if d == 0 else j_dn
        in_row = (j == RING - 1) if d == 0 else (j != 0)
        core = jnp.where(in_row, p, b)
        sub = jnp.where(in_row, b, p)
        return remote(
            ns.at[d, g, b], nr.at[d, g, sub], s_n.at[d, b, g], r_n.at[d, sub, g], dev(r, col, core)
        )

    def near_recv(d, b, g):
        return remote(ns.at[d, g, b], nr.at[d, g, b], s_n.at[d, b, g], r_n.at[d, b, g], up)

    def back_copy(b, g):
        return remote(xs.at[g, b], xr.at[g, p], s_b.at[b, g], r_b.at[p, g], dev(r_nx, j, b))

    def back_recv(b, g):
        return remote(xs.at[g, b], xr.at[g, b], s_b.at[b, g], r_b.at[b, g], dev(r_nx, j, b))

    def diag_copy(g):
        return remote(gs.at[g], gr.at[g], s_g.at[g], r_g.at[g], sib)

    def out_local(n, g):
        return pltpu.make_async_copy(
            dkv.at[g, n, my_rows], (dkc, dvc)[n].at[:, cols(p, g)], s_ol.at[n, g]
        )

    def out_remote(n, g):
        return remote(
            dkv.at[g, n, other_rows], (dkc, dvc)[n].at[:, cols(p, g)], s_or.at[n, g],
            r_or.at[n, g], sib,
        )

    def out_recv(n, g):
        return remote(
            dkv.at[g, n, other_rows], (dkc, dvc)[n].at[:, cols(1 - p, g)], s_or.at[n, g],
            r_or.at[n, g], sib,
        )

    def mine_copy(n):
        return pltpu.make_async_copy((q, do, kn, vn)[n], mine.at[n], s_mine.at[n])

    def noised_out(n):
        return pltpu.make_async_copy(on.at[n], (dkn, dvn)[n], s_on.at[n])

    def dq_out(plane, g):
        return pltpu.make_async_copy(dqs.at[:, cols(plane, g)], dq.at[:, cols(plane, g)], s_dq.at[plane, g])

    def grads(query, grad_out, keys, values, bias, deltas):
        s = dot_nt(keys, query)
        dp = dot_nt(values, grad_out)
        x = jnp.concatenate(
            [s[n * BLK : (n + 1) * BLK] * (SCALE * LOG2E) - row for n, row in enumerate(bias)], axis=0
        )
        prob = jnp.exp2(x)
        ds = (prob * (dp - deltas)).astype(BF16)
        return dot_tn(keys, ds), dot_nn(ds, query), dot_nn(prob.astype(BF16), grad_out)

    first_id = (me // 2) * 4

    def item(slot, b, g, c0, c1, first=False):
        ids = st[slot, b, 16:24, :]
        log_sums = st[slot, b, pl.ds(g, 1), :]
        bias = []
        for c in range(c0, c1):
            miss = jnp.min(jnp.abs(ids - (first_id + c).astype(F32)), axis=0, keepdims=True)
            bias.append(log_sums + jnp.minimum(miss, 1.0) * FAR_OFF)
        span = slice(c0 * BLK, c1 * BLK)
        d_q, d_k, d_v = grads(
            qd[slot, g, b, 0], qd[slot, g, b, 1], kv[g, 0, span], kv[g, 1, span],
            bias, st[slot, b, pl.ds(8 + g, 1), :],
        )
        if first:
            ak[span], av[span] = d_k, d_v
        else:
            ak[span] += d_k
            av[span] += d_v
        return d_q

    def own_pairs():
        for n in range(4):
            mine_copy(n).wait()

        def step(n, _):
            for h in (2 * n, 2 * n + 1):
                c = pl.ds(pl.multiple_of(h * HD, HD), HD)
                d_q, d_k, d_v = grads(
                    mine[0, :, c], mine[1, :, c], mine[2, :, c], mine[3, :, c],
                    [lse[pl.ds(h, 1), :] * LOG2E], delta[pl.ds(h, 1), :],
                )
                oq[h] = d_q
                on[0, :, c] = (d_k * SCALE).astype(BF16)
                on[1, :, c] = d_v.astype(BF16)
            return 0

        lax.fori_loop(0, nh, step, 0)
        for n in range(2):
            noised_out(n).start()

    def compute(g):
        odd = lax.rem(g, 2)
        near_p[0, odd, 0] = item(UP, 0, g, 0, 4, first=True)
        near_p[0, odd, 1] = item(UP, 1, g, 0, 4)
        diag = item(OWN, 1, g, 0, 2)

        @pl.when(p == 0)
        def _():
            gs[g] = diag.astype(BF16)
            diag_copy(g).start()

        @pl.when(p == 1)
        def _():
            oq[nh + g] += diag

        same_p[lax.rem(g, 4), 0] = item(SAME, 0, g, 0, 4)
        same_p[lax.rem(g, 4), 1] = item(SAME, 1, g, 2, 4)
        near_p[1, odd, 0] = item(DOWN, 0, g, 0, 4)
        near_p[1, odd, 1] = item(DOWN, 1, g, 0, 4)

    def compute_far(g):
        for b in range(2):
            fs[g, b] = item(FAR, b, g, 0, 4).astype(BF16)
        far_copy(g).start()
        dkv[g, 0] = (ak[...] * SCALE).astype(BF16)
        dkv[g, 1] = av[...].astype(BF16)
        for n in range(2):
            out_local(n, g).start()
            out_remote(n, g).start()

    def send_near(g):
        odd = lax.rem(g, 2)
        for d in range(2):

            @pl.when(middle)
            def _():
                far_recv(d, g).wait_recv()
                for b in range(2):
                    ns[d, g, b] = (near_p[d, odd, b] + fr[d, g, b].astype(F32)).astype(BF16)

            @pl.when(jnp.logical_not(middle))
            def _():
                for b in range(2):
                    ns[d, g, b] = near_p[d, odd, b].astype(BF16)

            for b in range(2):
                near_copy(d, b, g).start()

    def send_back(g):
        for d in range(2):
            for b in range(2):
                near_recv(d, b, g).wait_recv()
        for b in range(2):
            total = (
                same_p[lax.rem(g, 4), b]
                + jnp.where(j <= RING - 2, nr[1, g, b].astype(F32), 0.0)
                + jnp.where(j == 0, nr[0, g, b].astype(F32), 0.0)
            )
            xs[g, b] = total.astype(BF16)
            back_copy(b, g).start()

    def finish(g):
        @pl.when(p == 1)
        def _():
            diag_copy(g).wait_recv()
            oq[g] += gr[g].astype(F32)

        for plane in range(2):
            back_recv(plane, g).wait_recv()
            total = (
                oq[plane * nh + g]
                + xr[g, plane].astype(F32)
                + jnp.where(j >= 1, nr[0, g, plane].astype(F32), 0.0)
                + jnp.where(j == RING - 1, nr[1, g, plane].astype(F32), 0.0)
            )
            dqs[:, cols(plane, g)] = (total * SCALE).T.astype(BF16)
            dq_out(plane, g).start()

    for n in range(4):
        mine_copy(n).start()
    for plane in range(2):
        ms[plane, 0:nh] = lse[plane * nh : (plane + 1) * nh] * LOG2E
        ms[plane, 8 : 8 + nh] = delta[plane * nh : (plane + 1) * nh]
        for n in range(8):
            ms[plane, 16 + n : 17 + n] = jnp.full((1, BLK), listed[0, n].astype(F32))
    st[OWN, p] = ms[p]

    barrier = pltpu.get_barrier_semaphore()
    greeted = [sib] + [
        dev(a, b, c)
        for a, b in ((r, j_up), (r, j_dn), (r_nx, j), (r_pv, j))
        for c in range(2)
    ]
    for other in greeted:
        pl.semaphore_signal(
            barrier, inc=1, device_id=(other,), device_id_type=pl.DeviceIdType.MESH
        )
    pl.semaphore_wait(barrier, len(greeted))

    def stats_swap(blk):
        return remote(ms.at[1 - p], st.at[OWN, blk], s_sd.at[0], r_sd.at[0], sib)

    stats_swap(p).start()
    ahead = min(3, nh)
    for g in range(ahead):
        swap_start(g)
    stats_swap(1 - p).wait_recv()
    stats.send_own()
    for g in range(ahead):
        swap_wait(g)
        load(g).send_own()
    if ahead < nh:
        swap_start(ahead)
    stats.send_same()
    load(0).send_same()
    own_pairs()
    stats.relay()
    load(0).relay()
    if nh > 1:
        load(1).send_same()
    stats.far_wait()

    def step(t, _):
        @pl.when(t + 4 < nh)
        def _():
            swap_start(t + 4)

        @pl.when(t + 3 < nh)
        def _():
            swap_wait(t + 3)
            load(t + 3).send_own()

        @pl.when(t < nh)
        def _():
            compute(t)

        @pl.when(t + 2 < nh)
        def _():
            load(t + 2).send_same()

        @pl.when(t + 1 < nh)
        def _():
            load(t + 1).relay()

        @pl.when(t < nh)
        def _():
            load(t).far_wait()
            compute_far(t)

        @pl.when(jnp.logical_and(t >= 1, t < nh + 1))
        def _():
            send_near(t - 1)

        @pl.when(jnp.logical_and(t >= 2, t < nh + 2))
        def _():
            send_back(t - 2)

        @pl.when(t >= 3)
        def _():
            finish(t - 3)

        return 0

    lax.fori_loop(0, nh + 3, step, 0)

    stats_swap(p).wait_send()
    stats.done()
    for n in range(2):
        noised_out(n).wait()

    def drain(g, _):
        swap_done(g)
        load(g).done()
        far_copy(g).wait_send()
        for d in range(2):
            for b in range(2):
                near_copy(d, b, g).wait_send()
        for b in range(2):
            back_copy(b, g).wait_send()
            dq_out(b, g).wait()
            out_local(b, g).wait()
            out_remote(b, g).wait_send()
            out_recv(b, g).wait_recv()
        pl.when(p == 0)(lambda: diag_copy(g).wait_send())
        return 0

    lax.fori_loop(0, nh, drain, 0)


def per_device(rows, q_noised, k_noised, v_noised, dout, lse, delta, listed, k_clean, v_clean):
    width = q_noised.shape[1]
    nh = width // HD // 2
    vm, dma = pltpu.VMEM, pltpu.SemaphoreType.DMA
    hbm = pl.BlockSpec(memory_space=pl.ANY)
    tile = (HD, BLK)
    scratch = [
        vm((5, nh, 2, 2, BLK, HD), BF16),
        vm((nh, 2, KEYS, HD), BF16),
        vm((2, STAT, BLK), F32),
        vm((5, 2, STAT, BLK), F32),
        vm((4, BLK, width), BF16),
        vm((2 * nh, *tile), F32),
        vm((2, 2, 2, *tile), F32),
        vm((4, 2, *tile), F32),
        vm((KEYS, HD), F32),
        vm((KEYS, HD), F32),
        vm((nh, 2, KEYS, HD), BF16),
        vm((nh, 2, *tile), BF16),
        vm((2, nh, 2, *tile), BF16),
        vm((2, nh, 2, *tile), BF16),
        vm((2, nh, 2, *tile), BF16),
        vm((nh, 2, *tile), BF16),
        vm((nh, 2, *tile), BF16),
        vm((nh, *tile), BF16),
        vm((nh, *tile), BF16),
        vm((2, BLK, width), BF16),
        vm((BLK, width), BF16),
        dma((4,)),
        dma((4, nh)),
        dma((4, nh)),
        dma((4, nh)),
        dma((1,)),
        dma((1,)),
        *[dma((nh + 1,)) for _ in range(6)],
        dma((2, nh + 1)),
        dma((2, nh + 1)),
        dma((2, nh + 1)),
        dma((nh,)),
        dma((2, nh)),
        dma((2, 2, nh)),
        dma((2, 2, nh)),
        dma((2, nh)),
        dma((2, nh)),
        dma((nh,)),
        dma((nh,)),
        dma((2, nh)),
        dma((2, nh)),
        dma((2, nh)),
        dma((2,)),
        dma((2, nh)),
    ]
    pairs = 17 * 2 * nh
    return pl.pallas_call(
        functools.partial(kernel, rows, nh),
        out_shape=[jax.ShapeDtypeStruct((BLK, width), BF16)] * 3
        + [jax.ShapeDtypeStruct((CLEAN, width), BF16)] * 2,
        in_specs=[hbm] * 6
        + [pl.BlockSpec(memory_space=pltpu.VMEM)] * 2
        + [pl.BlockSpec(memory_space=pltpu.SMEM)],
        out_specs=[hbm] * 5,
        scratch_shapes=scratch,
        compiler_params=pltpu.CompilerParams(
            collective_id=0, has_side_effects=True, vmem_limit_bytes=60 * 2**20
        ),
        cost_estimate=pl.CostEstimate(
            flops=pairs * 10 * BLK * BLK * HD,
            bytes_accessed=15 * 2**20,
            transcendentals=pairs * BLK * BLK,
        ),
        name="block_attention_backward",
    )(q_noised, dout, k_noised, v_noised, k_clean, v_clean, lse, delta, listed)


def solution(mesh):
    rows = mesh.shape["ctx"] // (2 * RING)
    split = P("ctx", None)
    return jax.shard_map(
        functools.partial(per_device, rows),
        mesh=mesh,
        in_specs=(split,) * 4 + (P(None, "ctx"),) * 2 + (split,) * 3,
        out_specs=(split,) * 5,
        check_vma=False,
    )
```

time: 533 us -> 159 us (0.30)
  waiting for transfers between devices: 186 us -> 0 us
  Pallas kernels: 0 us -> 149 us
  matrix products: 116 us -> 0 us
  local copies, waits for them, and re-layouts: 99.9 us -> 8.14 us
  other arithmetic: 64.6 us -> 0 us
  starting transfers between devices: 52.6 us -> 0 us
  loops' own time: 10.8 us -> 0 us
    ppermute x49 -> x0, waiting for transfers between devices: 186 us -> none  [from_behind(): return lax.ppermute(value, axis, pairs)]
    pallas_call x0 -> x1, Pallas kernels: none -> 149 us  [per_device(): pl.pallas_call(functools.partial(kernel, rows, nh), out_shape=[jax.ShapeD...]
    dot_general x85 -> x0, matrix products: 116 us -> none  [the longest x17 36.2 us: pair_grads(): jnp.einsum('qhd,khd->hqk', o_heads, v_heads, preferred_element_type=jnp.f...]
    ppermute x49 -> x0, starting transfers between devices: 52.6 us -> none  [from_behind(): return lax.ppermute(value, axis, pairs)]
    add x24 -> x0, other arithmetic: 45 us -> none  [the longest x8 24.9 us: cycle_step(): acc_q + part_q]
    while x187 -> x0, local copies, waits for them, and re-layouts: 43.3 us -> none
    slice x8 -> x0, local copies, waits for them, and re-layouts: 34.9 us -> none  [visit(): values = v_clean[slot * rows:(slot + 1) * rows]]
    while x8 -> x0, other arithmetic: 11.6 us -> none
  transfers between devices with their start and end apart: 49 -> 0, of which waited for: 17 -> 0; matrix products, arithmetic and copies ran while one was open for 42% -> 0% of each run, Pallas kernels for 0% -> 0%
where the time goes in v1:
time: 159 us; the launch traced here: 158 us
  Pallas kernels  149 us (94%)
  local copies, waits for them, and re-layouts  8.14 us (5%)
    pallas_call x1, Pallas kernels, per_device(): pl.pallas_call(functools.partial(kernel, rows, nh), out_shape=[jax.ShapeD...  149 us
    unnamed x13, local copies, waits for them, and re-layouts  8.14 us

profile of v1, /device:TPU:1, one launch (start us, length us, event | category | flops | bytes accessed | tf_op | source)
XLA Modules:
  0.0 158.1 jit_solution(7208910638329515812)
XLA Ops:
  0.6 149.3 %block_attention_backward.1 = (bf16[256,2048]{1,0:T(8,128)(2,1)}, bf16[256,2048]{1,0:T(8,128)(2,1)}, bf16[256,2048]{1,0:T(8,128)(2,1)}, bf16[512,2048]{1,0:T(8,128)(2,1)}, bf16[512,2048]{1,0:T(8,128)(2,1)}) custom-call(bf16[256,2048]{1,0:T(8,128)(2,1)} %q.1, bf16[256,2048]{1,0:T(8,128)(2,1)} %do.1, bf16[256,2048]{1,0:T(8,128)(2,1)} %kn.1, ...), custom_call_target="tpu_custom_call" | custom-call | flops 22817013760 | bytes 15728640 | tf_op jit(solution)/shard_map/block_attention_backward/pallas_call | solution.py:512
  149.9 0.0 copy-start.3
  149.9 0.0 copy-start.2
  149.9 2.5 %copy.19 = bf16[256,2048]{1,0:T(8,128)(2,1)} copy(bf16[256,2048]{1,0:T(8,128)(2,1)} %get-tuple-element.10) | data formatting | bytes 2097152
  152.4 0.0 copy-done.3
  152.4 0.0 copy-start.1
  152.4 1.0 copy.20
  153.4 0.0 copy-done.2
  153.4 1.0 copy.21
  154.3 0.1 copy-done.1
  154.4 0.0 copy-start
  154.4 1.3 copy.22
  155.7 1.0 copy-done
  156.8 1.3 copy.23
Async XLA Ops:
  149.9 2.5 %copy-start.3 = (bf16[256,2048]{1,0:T(8,128)(2,1)S(1)}, bf16[256,2048]{1,0:T(8,128)(2,1)}, u32[]{:S(2)}) copy-start(bf16[256,2048]{1,0:T(8,128)(2,1)} %get-tuple-element.11) | copy-start | bytes 3145732
  149.9 3.4 %copy-start.2 = (bf16[256,2048]{1,0:T(8,128)(2,1)S(1)}, bf16[256,2048]{1,0:T(8,128)(2,1)}, u32[]{:S(2)}) copy-start(bf16[256,2048]{1,0:T(8,128)(2,1)} %get-tuple-element.12) | copy-start | bytes 3145732
  152.4 2.0 %copy-start.1 = (bf16[512,2048]{1,0:T(8,128)(2,1)S(1)}, bf16[512,2048]{1,0:T(8,128)(2,1)}, u32[]{:S(2)}) copy-start(bf16[512,2048]{1,0:T(8,128)(2,1)} %get-tuple-element.13) | copy-start | bytes 6291460
  154.4 2.3 %copy-start = (bf16[512,2048]{1,0:T(8,128)(2,1)S(1)}, bf16[512,2048]{1,0:T(8,128)(2,1)}, u32[]{:S(2)}) copy-start(bf16[512,2048]{1,0:T(8,128)(2,1)} %get-tuple-element.14) | copy-start | bytes 6291460

commit v2 on v1

v2 whole, which is shorter than its diff:
```python
import functools

import jax
import jax.numpy as jnp
from jax import lax
from jax.experimental import pallas as pl
from jax.experimental.pallas import tpu as pltpu
from jax.sharding import PartitionSpec as P

F32 = jnp.float32
BF16 = jnp.bfloat16
HD = 128
BLK = 256
CLEAN = 512
RING = 4
SCALE = HD**-0.5
LOG2E = 1.4426950408889634
FAR_OFF = 1e30
STAT = 24

OWN, UP, DOWN, FAR = range(4)
HERE, BEFORE = range(2)


def dot_nt(a, b):
    return lax.dot_general(a, b, (((1,), (1,)), ((), ())), preferred_element_type=F32)


def dot_nn(a, b):
    return lax.dot_general(a, b, (((1,), (0,)), ((), ())), preferred_element_type=F32)


def dot_tn(a, b):
    return lax.dot_general(a, b, (((0,), (0,)), ((), ())), preferred_element_type=F32)


def kernel(
    rows, nh,
    q, do, kn, vn, kc, vc, lse, delta, listed,
    dq, dkn, dvn, dkc, dvc,
    qd, kv, lv, dv, ms, st, mine, oq, part, near_p, acc, db, dr, fs, fr, ns, nr, gs, gr, dqs,
    s_in, s_mine, s_loc, s_d2d, r_d2d, s_sd, r_sd, s_kb, r_kb,
    s_dn, r_dn, s_up, r_up, s_rd, s_ru, r_far,
    s_f, r_f, s_n, r_n, s_b, r_b, s_g, r_g, s_ol, s_or, r_or, s_on, s_dq,
):
    me = lax.axis_index("ctx")
    p = lax.rem(me, 2)
    j = lax.rem(me // 2, RING)
    r = me // (2 * RING)

    def dev(row, col, core):
        return row * (2 * RING) + col * 2 + core

    j_up, j_dn = lax.rem(j + 1, RING), lax.rem(j + RING - 1, RING)
    r_nx, r_pv = lax.rem(r + 1, rows), lax.rem(r + rows - 1, rows)
    sib = dev(r, j, 1 - p)
    up, dn, nxt, prev = dev(r, j_up, p), dev(r, j_dn, p), dev(r_nx, j, p), dev(r_pv, j, p)

    set_up = jnp.where(j < RING - 1, HERE, BEFORE)
    set_down = jnp.where(j > 0, BEFORE, HERE)
    set_far = jnp.where(j < RING // 2, HERE, BEFORE)

    def remote(src, dst, ss, rs, to):
        return pltpu.make_async_remote_copy(
            src_ref=src, dst_ref=dst, send_sem=ss, recv_sem=rs,
            device_id=(to,), device_id_type=pl.DeviceIdType.MESH,
        )

    def cols(plane, g):
        return pl.ds(pl.multiple_of((plane * nh + g) * HD, HD), HD)

    def swap_place(n, g, core):
        return qd.at[OWN, g, core, n] if n < 2 else kv.at[g, HERE, core, n - 2]

    def swap_local(n, g):
        return pltpu.make_async_copy(
            (q, do, kc, vc)[n].at[:, cols(p, g)], swap_place(n, g, p), s_loc.at[n, g]
        )

    def swap_send(n, g):
        return remote(
            (q, do, kc, vc)[n].at[:, cols(1 - p, g)], swap_place(n, g, p), s_d2d.at[n, g],
            r_d2d.at[n, g], sib,
        )

    def swap_recv(n, g):
        return remote(
            (q, do, kc, vc)[n].at[:, cols(1 - p, g)], swap_place(n, g, 1 - p), s_d2d.at[n, g],
            r_d2d.at[n, g], sib,
        )

    queries, clean = (0, 1), (2, 3)

    def swap_start(which, g):
        for n in which:
            swap_send(n, g).start()
        for n in which:
            swap_local(n, g).start()

    def swap_wait(which, g):
        for n in which:
            swap_local(n, g).wait()
            swap_recv(n, g).wait_recv()

    def keys_on(h, g):
        return remote(kv.at[g, HERE, h], kv.at[g, BEFORE, h], s_kb.at[h, g], r_kb.at[h, g], nxt)

    class Load:
        def __init__(self, ref, i, stats):
            self.i = i
            self.at = (lambda s: ref.at[s]) if stats else (lambda s: ref.at[s, i])
            self.blk = (lambda s, b: ref.at[s, b]) if stats else (lambda s, b: ref.at[s, i, b])

        def down(self):
            return remote(self.at(OWN), self.at(UP), s_dn.at[self.i], r_dn.at[self.i], dn)

        def up(self):
            return remote(self.at(OWN), self.at(DOWN), s_up.at[self.i], r_up.at[self.i], up)

        def relay_down(self):
            return remote(self.blk(UP, 0), self.blk(FAR, 0), s_rd.at[self.i], r_far.at[0, self.i], dn)

        def relay_up(self):
            return remote(self.blk(DOWN, 1), self.blk(FAR, 1), s_ru.at[self.i], r_far.at[1, self.i], up)

        def send_own(self):
            self.down().start()
            self.up().start()

        def relay(self):
            self.down().wait_recv()
            self.relay_down().start()
            self.up().wait_recv()
            self.relay_up().start()

        def far_wait(self):
            self.relay_down().wait_recv()
            self.relay_up().wait_recv()

        def done(self):
            self.down().wait_send()
            self.up().wait_send()
            self.relay_down().wait_send()
            self.relay_up().wait_send()

    def load(g):
        return Load(qd, g, False)

    stats = Load(st, nh, True)

    def far_copy(d, g):
        return remote(fs.at[d, g], fr.at[d, g], s_f.at[d, g], r_f.at[d, g], (up, dn)[d])

    def near_copy(d, b, g):
        return remote(
            ns.at[d, g, b], nr.at[d, g, p], s_n.at[d, b, g], r_n.at[d, p, g],
            dev(r, (j_up, j_dn)[d], b),
        )

    def near_recv(d, plane, g):
        return remote(
            ns.at[d, g, plane], nr.at[d, g, plane], s_n.at[d, plane, g], r_n.at[d, plane, g], up
        )

    def back_copy(h, g):
        return remote(db.at[g, h], dr.at[g, h], s_b.at[h, g], r_b.at[h, g], prev)

    def own_copy(g):
        return remote(gs.at[g], gr.at[g], s_g.at[g], r_g.at[g], sib)

    def out_local(n, g):
        return pltpu.make_async_copy(
            dr.at[g, p, n], (dkc, dvc)[n].at[:, cols(p, g)], s_ol.at[n, g]
        )

    def out_remote(n, g):
        return remote(
            dr.at[g, 1 - p, n], (dkc, dvc)[n].at[:, cols(p, g)], s_or.at[n, g], r_or.at[n, g], sib
        )

    def out_recv(n, g):
        return remote(
            dr.at[g, p, n], (dkc, dvc)[n].at[:, cols(1 - p, g)], s_or.at[n, g], r_or.at[n, g], sib
        )

    def mine_copy(n):
        return pltpu.make_async_copy((q, do, kn, vn)[n], mine.at[n], s_mine.at[n])

    def noised_out(n, plane, g):
        c = cols(plane, g)
        return pltpu.make_async_copy(
            mine.at[2 + n, :, c], (dkn, dvn)[n].at[:, c], s_on.at[n, plane, g]
        )

    def dq_out(plane, g):
        return pltpu.make_async_copy(
            dqs.at[:, cols(plane, g)], dq.at[:, cols(plane, g)], s_dq.at[plane, g]
        )

    def grads(query, grad_out, keys, values, bias, deltas):
        s = dot_nt(keys, query)
        dp = dot_nt(values, grad_out)
        x = jnp.concatenate(
            [s[n * BLK : (n + 1) * BLK] * (SCALE * LOG2E) - row for n, row in enumerate(bias)], axis=0
        )
        prob = jnp.exp2(x)
        ds = (prob * (dp - deltas)).astype(BF16)
        return dot_tn(keys, ds), dot_nn(ds, query), dot_nn(prob.astype(BF16), grad_out)

    first_here = (me // 2) * 4
    first_before = (r_pv * RING + j) * 4

    def item(slot, b, g, h, keys_set, first=False):
        first_id = jnp.where(keys_set == HERE, first_here, first_before) + 2 * h
        place = jnp.where(keys_set == HERE, lax.rem(2 * g + h, 4), 4)
        ids = st[slot, b, 16:24, :]
        log_sums = st[slot, b, pl.ds(g, 1), :]
        bias = []
        for c in range(2):
            miss = jnp.min(jnp.abs(ids - (first_id + c).astype(F32)), axis=0, keepdims=True)
            bias.append(log_sums + jnp.minimum(miss, 1.0) * FAR_OFF)
        d_q, d_k, d_v = grads(
            qd[slot, g, b, 0], qd[slot, g, b, 1], kv[g, keys_set, h, 0], kv[g, keys_set, h, 1],
            bias, st[slot, b, pl.ds(8 + g, 1), :],
        )
        if first:
            acc[place, 0], acc[place, 1] = d_k, d_v
        else:
            acc[place, 0] += d_k
            acc[place, 1] += d_v
        return d_q

    def own_pairs(g):
        for plane in range(2):
            h, c = plane * nh + g, cols(plane, g)
            d_q, d_k, d_v = grads(
                mine[0, :, c], mine[1, :, c], mine[2, :, c], mine[3, :, c],
                [lv[pl.ds(h, 1), :] * LOG2E], dv[pl.ds(h, 1), :],
            )
            oq[h] = d_q
            mine[2, :, c] = (d_k * SCALE).astype(BF16)
            mine[3, :, c] = d_v.astype(BF16)
        for n in range(2):
            for plane in range(2):
                noised_out(n, plane, g).start()

    def send_keys_grads(h, g):
        for n in range(2):
            db[g, h, n] = acc[4, n].astype(BF16)
        back_copy(h, g).start()

    def first_half(g):
        keys_on(0, g).wait_recv()

        @pl.when(g + 1 < nh)
        def _():
            swap_wait(clean, g + 1)
            keys_on(0, g + 1).start()

        part[OWN, 0] = item(OWN, 0, g, 0, BEFORE, first=True)
        part[OWN, 1] = item(OWN, 1, g, 0, HERE, first=True)
        for b in range(2):
            part[DOWN, b] = item(DOWN, b, g, 0, set_down)
        for b in range(2):
            part[UP, b] = item(UP, b, g, 0, set_up)

        @pl.when(g >= 1)
        def _():
            send_near(g - 1)

        @pl.when(g == 0)
        def _():
            stats.far_wait()

        load(g).far_wait()
        for b in range(2):
            part[FAR, b] = item(FAR, b, g, 0, set_far)
        send_keys_grads(0, g)

    def second_half(g):
        keys_on(1, g).wait_recv()

        @pl.when(g + 1 < nh)
        def _():
            keys_on(1, g + 1).start()

        for n in range(2):
            acc[lax.rem(2 * g + 1, 4), n] = jnp.zeros((CLEAN, HD), F32)
        own_0 = part[OWN, 0] + item(OWN, 0, g, 1, BEFORE, first=True)
        for b in range(2):
            fs[b, g] = (part[FAR, b] + item(FAR, b, g, 1, set_far)).astype(BF16)
        for d in range(2):
            far_copy(d, g).start()

        @pl.when(g + 2 < nh)
        def _():
            swap_wait(queries, g + 2)
            load(g + 2).send_own()

        own_1 = part[OWN, 1] + item(OWN, 1, g, 1, BEFORE)
        oq[p * nh + g] += jnp.where(p == 0, own_0, own_1)
        gs[g] = jnp.where(p == 0, own_1, own_0).astype(BF16)
        own_copy(g).start()
        ns[1, g, 0] = (part[DOWN, 0] + item(DOWN, 0, g, 1, set_down)).astype(BF16)
        near_copy(1, 0, g).start()
        near_p[1] = part[DOWN, 1] + item(DOWN, 1, g, 1, set_down)
        ns[0, g, 1] = (part[UP, 1] + item(UP, 1, g, 1, set_up)).astype(BF16)
        near_copy(0, 1, g).start()
        near_p[0] = part[UP, 0] + item(UP, 0, g, 1, set_up)
        send_keys_grads(1, g)

    def send_near(g):
        for d in range(2):
            far_copy(d, g).wait_recv()
            ns[d, g, d] = (near_p[d] + fr[d, g].astype(F32)).astype(BF16)
            near_copy(d, d, g).start()

    def finish_clean(h, g):
        back_copy(h, g).wait_recv()
        for n in range(2):
            total = acc[lax.rem(2 * g + h, 4), n] + dr[g, h, n].astype(F32)
            dr[g, h, n] = (total * (SCALE if n == 0 else 1.0)).astype(BF16)

        @pl.when(p == h)
        def _():
            for n in range(2):
                out_local(n, g).start()

        @pl.when(p != h)
        def _():
            for n in range(2):
                out_remote(n, g).start()

    def finish(g):
        own_copy(g).wait_recv()
        oq[(1 - p) * nh + g] += gr[g].astype(F32)
        for plane in range(2):
            for d in range(2):
                near_recv(d, plane, g).wait_recv()
            total = oq[plane * nh + g] + nr[0, g, plane].astype(F32) + nr[1, g, plane].astype(F32)
            dqs[:, cols(plane, g)] = (total * SCALE).T.astype(BF16)
            dq_out(plane, g).start()

    def drain(g):
        for n in range(4):
            swap_send(n, g).wait_send()
        load(g).done()
        own_copy(g).wait_send()
        for n in range(2):
            for m in range(2):
                near_copy(n, m, g).wait_send()
                noised_out(n, m, g).wait()
            keys_on(n, g).wait_send()
            far_copy(n, g).wait_send()
            back_copy(n, g).wait_send()
            dq_out(n, g).wait()
            out_local(n, g).wait()
            out_remote(n, g).wait_send()
            out_recv(n, g).wait_recv()

    barrier = pltpu.get_barrier_semaphore()
    greeted = [sib, nxt, prev] + [dev(r, col, core) for col in (j_up, j_dn) for core in range(2)]
    for other in greeted:
        pl.semaphore_signal(
            barrier, inc=1, device_id=(other,), device_id_type=pl.DeviceIdType.MESH
        )
    in_lse = pltpu.make_async_copy(lse, lv, s_in.at[0])
    in_delta = pltpu.make_async_copy(delta, dv, s_in.at[1])
    in_lse.start()
    in_delta.start()

    def stats_swap(blk):
        return remote(ms.at[1 - p], st.at[OWN, blk], s_sd.at[0], r_sd.at[0], sib)

    pl.semaphore_wait(barrier, len(greeted))
    swap_start(queries, 0)
    swap_start(clean, 0)
    in_lse.wait()
    in_delta.wait()
    for plane in range(2):
        ms[plane, 0:nh] = lv[plane * nh : (plane + 1) * nh] * LOG2E
        ms[plane, 8 : 8 + nh] = dv[plane * nh : (plane + 1) * nh]
        for n in range(8):
            ms[plane, 16 + n : 17 + n] = jnp.full((1, BLK), listed[0, n].astype(F32))
    st[OWN, p] = ms[p]
    stats_swap(p).start()
    swap_wait(queries, 0)
    load(0).send_own()
    swap_wait(clean, 0)
    keys_on(0, 0).start()
    stats_swap(1 - p).wait_recv()
    stats.send_own()
    for g in range(1, min(3, nh)):
        swap_start(queries, g)
    for g in range(1, min(2, nh)):
        swap_start(clean, g)
    for n in range(4):
        mine_copy(n).start()
    load(0).relay()
    stats.relay()
    keys_on(1, 0).start()
    if nh > 1:
        swap_wait(queries, 1)
        load(1).send_own()

    def step(t, _):
        @pl.when(t + 3 < nh)
        def _():
            swap_start(queries, t + 3)

        @pl.when(t + 2 < nh)
        def _():
            swap_start(clean, t + 2)

        first_half(t)

        @pl.when(t == 0)
        def _():
            for n in range(4):
                mine_copy(n).wait()

        own_pairs(t)

        @pl.when(t + 1 < nh)
        def _():
            load(t + 1).relay()

        second_half(t)

        @pl.when(t >= 1)
        def _():
            finish_clean(0, t - 1)
            finish_clean(1, t - 1)

        @pl.when(t >= 2)
        def _():
            finish(t - 2)

        @pl.when(t >= 3)
        def _():
            drain(t - 3)

        return 0

    lax.fori_loop(0, nh, step, 0)
    send_near(nh - 1)
    finish_clean(0, nh - 1)
    finish_clean(1, nh - 1)
    if nh > 1:
        finish(nh - 2)
    finish(nh - 1)

    stats_swap(p).wait_send()
    stats.done()
    for g in range(max(nh - 3, 0), nh):
        drain(g)


def copy_out(*refs):
    sources, results, held, arrive, leave = refs[:5], refs[5:10], refs[10:15], refs[15], refs[16]
    into, out = [], []
    for n in range(5):
        rows = sources[n].shape[0] // 2
        for k in range(2):
            span = pl.ds(k * rows, rows)
            into.append(pltpu.make_async_copy(sources[n].at[span], held[n].at[span], arrive.at[n, k]))
            out.append(pltpu.make_async_copy(held[n].at[span], results[n].at[span], leave.at[n, k]))
    for copy in into:
        copy.start()
    for one, two in zip(into, out, strict=True):
        one.wait()
        two.start()
    for copy in out:
        copy.wait()


def per_device(rows, q_noised, k_noised, v_noised, dout, lse, delta, listed, k_clean, v_clean):
    width = q_noised.shape[1]
    nh = width // HD // 2
    vm, dma = pltpu.VMEM, pltpu.SemaphoreType.DMA
    hbm = pl.BlockSpec(memory_space=pl.ANY)
    tile = (HD, BLK)
    scratch = [
        vm((4, nh, 2, 2, BLK, HD), BF16),
        vm((nh, 2, 2, 2, CLEAN, HD), BF16),
        vm((2 * nh, BLK), F32),
        vm((2 * nh, BLK), F32),
        vm((2, STAT, BLK), F32),
        vm((4, 2, STAT, BLK), F32),
        vm((4, BLK, width), BF16),
        vm((2 * nh, *tile), F32),
        vm((4, 2, *tile), F32),
        vm((2, *tile), F32),
        vm((5, 2, CLEAN, HD), F32),
        vm((nh, 2, 2, CLEAN, HD), BF16),
        vm((nh, 2, 2, CLEAN, HD), BF16),
        vm((2, nh, *tile), BF16),
        vm((2, nh, *tile), BF16),
        vm((2, nh, 2, *tile), BF16),
        vm((2, nh, 2, *tile), BF16),
        vm((nh, *tile), BF16),
        vm((nh, *tile), BF16),
        vm((BLK, width), BF16),
        dma((2,)),
        dma((4,)),
        dma((4, nh)),
        dma((4, nh)),
        dma((4, nh)),
        dma((1,)),
        dma((1,)),
        dma((2, nh)),
        dma((2, nh)),
        *[dma((nh + 1,)) for _ in range(6)],
        dma((2, nh + 1)),
        dma((2, nh)),
        dma((2, nh)),
        dma((2, 2, nh)),
        dma((2, 2, nh)),
        dma((2, nh)),
        dma((2, nh)),
        dma((nh,)),
        dma((nh,)),
        dma((2, nh)),
        dma((2, nh)),
        dma((2, nh)),
        dma((2, 2, nh)),
        dma((2, nh)),
    ]
    pairs = 17 * 2 * nh
    outs = pl.pallas_call(
        functools.partial(kernel, rows, nh),
        out_shape=[jax.ShapeDtypeStruct((BLK, width), BF16)] * 3
        + [jax.ShapeDtypeStruct((CLEAN, width), BF16)] * 2,
        in_specs=[hbm] * 8 + [pl.BlockSpec(memory_space=pltpu.SMEM)],
        out_specs=[hbm] * 5,
        scratch_shapes=scratch,
        compiler_params=pltpu.CompilerParams(
            collective_id=0, has_side_effects=True, vmem_limit_bytes=60 * 2**20
        ),
        cost_estimate=pl.CostEstimate(
            flops=pairs * 10 * BLK * BLK * HD,
            bytes_accessed=15 * 2**20,
            transcendentals=pairs * BLK * BLK,
        ),
        name="block_attention_backward",
    )(q_noised, dout, k_noised, v_noised, k_clean, v_clean, lse, delta, listed)
    return pl.pallas_call(
        copy_out,
        out_shape=[jax.ShapeDtypeStruct(out.shape, out.dtype) for out in outs],
        in_specs=[hbm] * 5,
        out_specs=[hbm] * 5,
        scratch_shapes=[vm(out.shape, out.dtype) for out in outs] + [dma((5, 2)), dma((5, 2))],
        name="copy_out",
    )(*outs)


def solution(mesh):
    rows = mesh.shape["ctx"] // (2 * RING)
    split = P("ctx", None)
    return jax.shard_map(
        functools.partial(per_device, rows),
        mesh=mesh,
        in_specs=(split,) * 4 + (P(None, "ctx"),) * 2 + (split,) * 3,
        out_specs=(split,) * 5,
        check_vma=False,
    )
```

time: 159 us -> 136 us (0.86)
  Pallas kernels: 149 us -> 134 us
  local copies, waits for them, and re-layouts: 8.14 us -> 0 us
    pallas_call x1, Pallas kernels: 149 us -> 128 us  [per_device(): pl.pallas_call(functools.partial(kernel, rows, nh), out_shape=[jax.ShapeD...]
    unnamed x13 -> x0, local copies, waits for them, and re-layouts: 8.14 us -> none
    pallas_call x0 -> x1, Pallas kernels: none -> 5.81 us  [per_device(): pl.pallas_call(copy_out, out_shape=[jax.ShapeDtypeStruct(out.shape, out.d...]
where the time goes in v2:
time: 136 us; the launch traced here: 135 us
  Pallas kernels  134 us (99%)
    pallas_call x1, Pallas kernels, per_device(): pl.pallas_call(functools.partial(kernel, rows, nh), out_shape=[jax.ShapeD...  128 us
    pallas_call x1, Pallas kernels, per_device(): pl.pallas_call(copy_out, out_shape=[jax.ShapeDtypeStruct(out.shape, out.d...  5.81 us

profile of v2, /device:TPU:1, one launch (start us, length us, event | category | flops | bytes accessed | tf_op | source)
XLA Modules:
  0.0 134.9 jit_solution(8837850239737328637)
XLA Ops:
  0.6 128.4 %block_attention_backward.1 = (bf16[256,2048]{1,0:T(8,128)(2,1)}, bf16[256,2048]{1,0:T(8,128)(2,1)}, bf16[256,2048]{1,0:T(8,128)(2,1)}, bf16[512,2048]{1,0:T(8,128)(2,1)}, bf16[512,2048]{1,0:T(8,128)(2,1)}) custom-call(bf16[256,2048]{1,0:T(8,128)(2,1)} %q.1, bf16[256,2048]{1,0:T(8,128)(2,1)} %do.1, bf16[256,2048]{1,0:T(8,128)(2,1)} %kn.1, ...), custom_call_target="tpu_custom_call" | custom-call | flops 22817013760 | bytes 15728640 | tf_op jit(solution)/shard_map/block_attention_backward/pallas_call | solution.py:530
  129.1 5.8 %copy_out.1 = (bf16[256,2048]{1,0:T(8,128)(2,1)}, bf16[256,2048]{1,0:T(8,128)(2,1)}, bf16[256,2048]{1,0:T(8,128)(2,1)}, bf16[512,2048]{1,0:T(8,128)(2,1)}, bf16[512,2048]{1,0:T(8,128)(2,1)}) custom-call(bf16[256,2048]{1,0:T(8,128)(2,1)} %get-tuple-element.10.refs_0_, bf16[256,2048]{1,0:T(8,128)(2,1)} %get-tuple-element.11.refs_1_, ...), custom_call_target="tpu_custom_call" | custom-call | tf_op jit(solution)/shard_map/copy_out/pallas_call | solution.py:547

commit v3 on v2

--- a/solution.py
+++ b/solution.py
@@ -39,7 +39,8 @@
     q, do, kn, vn, kc, vc, lse, delta, listed,
     dq, dkn, dvn, dkc, dvc,
     qd, kv, lv, dv, ms, st, mine, oq, part, near_p, acc, db, dr, fs, fr, ns, nr, gs, gr, dqs,
-    s_in, s_mine, s_loc, s_d2d, r_d2d, s_sd, r_sd, s_kb, r_kb,
+    lm, s_in, s_mine, s_loc, s_d2d, r_d2d, s_sd, r_sd, s_kb, r_kb,
+    s_q0, r_q0, s_k0, r_k0,
     s_dn, r_dn, s_up, r_up, s_rd, s_ru, r_far,
     s_f, r_f, s_n, r_n, s_b, r_b, s_g, r_g, s_ol, s_or, r_or, s_on, s_dq,
 ):
@@ -105,6 +106,40 @@
     def keys_on(h, g):
         return remote(kv.at[g, HERE, h], kv.at[g, BEFORE, h], s_kb.at[h, g], r_kb.at[h, g], nxt)
 
+    def first_query(d, plane, n):
+        return remote(
+            (q, do)[n].at[:, cols(plane, 0)], qd.at[(UP, DOWN)[d], 0, p, n],
+            s_q0.at[d, plane, n], r_q0.at[d, p, n], dev(r, (j_dn, j_up)[d], plane),
+        )
+
+    def first_query_recv(d, core, n):
+        return remote(
+            (q, do)[n].at[:, cols(core, 0)], qd.at[(UP, DOWN)[d], 0, core, n],
+            s_q0.at[d, core, n], r_q0.at[d, core, n], up,
+        )
+
+    def first_keys(plane, n):
+        return remote(
+            (kc, vc)[n].at[:, cols(plane, 0)], kv.at[0, BEFORE, p, n],
+            s_k0.at[plane, n], r_k0.at[p, n], dev(r_nx, j, plane),
+        )
+
+    def first_keys_recv(core, n):
+        return remote(
+            (kc, vc)[n].at[:, cols(core, 0)], kv.at[0, BEFORE, core, n],
+            s_k0.at[core, n], r_k0.at[core, n], nxt,
+        )
+
+    def keys_wait(h, g):
+        @pl.when(g == 0)
+        def _():
+            for n in range(2):
+                first_keys_recv(h, n).wait_recv()
+
+        @pl.when(g > 0)
+        def _():
+            keys_on(h, g).wait_recv()
+
     class Load:
         def __init__(self, ref, i, stats):
             self.i = i
@@ -137,9 +172,11 @@
             self.relay_down().wait_recv()
             self.relay_up().wait_recv()
 
-        def done(self):
+        def done_own(self):
             self.down().wait_send()
             self.up().wait_send()
+
+        def done(self):
             self.relay_down().wait_send()
             self.relay_up().wait_send()
 
@@ -250,7 +287,7 @@
         back_copy(h, g).start()
 
     def first_half(g):
-        keys_on(0, g).wait_recv()
+        keys_wait(0, g)
 
         @pl.when(g + 1 < nh)
         def _():
@@ -264,9 +301,9 @@
         for b in range(2):
             part[UP, b] = item(UP, b, g, 0, set_up)
 
-        @pl.when(g >= 1)
-        def _():
-            send_near(g - 1)
+        @pl.when(g >= 2)
+        def _():
+            send_near(g - 2)
 
         @pl.when(g == 0)
         def _():
@@ -278,7 +315,7 @@
         send_keys_grads(0, g)
 
     def second_half(g):
-        keys_on(1, g).wait_recv()
+        keys_wait(1, g)
 
         @pl.when(g + 1 < nh)
         def _():
@@ -303,16 +340,16 @@
         own_copy(g).start()
         ns[1, g, 0] = (part[DOWN, 0] + item(DOWN, 0, g, 1, set_down)).astype(BF16)
         near_copy(1, 0, g).start()
-        near_p[1] = part[DOWN, 1] + item(DOWN, 1, g, 1, set_down)
+        near_p[lax.rem(g, 2), 1] = part[DOWN, 1] + item(DOWN, 1, g, 1, set_down)
         ns[0, g, 1] = (part[UP, 1] + item(UP, 1, g, 1, set_up)).astype(BF16)
         near_copy(0, 1, g).start()
-        near_p[0] = part[UP, 0] + item(UP, 0, g, 1, set_up)
+        near_p[lax.rem(g, 2), 0] = part[UP, 0] + item(UP, 0, g, 1, set_up)
         send_keys_grads(1, g)
 
     def send_near(g):
         for d in range(2):
             far_copy(d, g).wait_recv()
-            ns[d, g, d] = (near_p[d] + fr[d, g].astype(F32)).astype(BF16)
+            ns[d, g, d] = (near_p[lax.rem(g, 2), d] + fr[d, g].astype(F32)).astype(BF16)
             near_copy(d, d, g).start()
 
     def finish_clean(h, g):
@@ -345,12 +382,26 @@
         for n in range(4):
             swap_send(n, g).wait_send()
         load(g).done()
+
+        @pl.when(g > 0)
+        def _():
+            load(g).done_own()
+            for h in range(2):
+                keys_on(h, g).wait_send()
+
+        @pl.when(g == 0)
+        def _():
+            for plane in range(2):
+                for n in range(2):
+                    first_keys(plane, n).wait_send()
+                    for d in range(2):
+                        first_query(d, plane, n).wait_send()
+
         own_copy(g).wait_send()
         for n in range(2):
             for m in range(2):
                 near_copy(n, m, g).wait_send()
                 noised_out(n, m, g).wait()
-            keys_on(n, g).wait_send()
             far_copy(n, g).wait_send()
             back_copy(n, g).wait_send()
             dq_out(n, g).wait()
@@ -359,35 +410,41 @@
             out_recv(n, g).wait_recv()
 
     barrier = pltpu.get_barrier_semaphore()
-    greeted = [sib, nxt, prev] + [dev(r, col, core) for col in (j_up, j_dn) for core in range(2)]
+    greeted = [sib, nxt, prev, dev(r_nx, j, 1 - p), dev(r_pv, j, 1 - p)] + [dev(r, col, core) for col in (j_up, j_dn) for core in range(2)]
     for other in greeted:
         pl.semaphore_signal(
             barrier, inc=1, device_id=(other,), device_id_type=pl.DeviceIdType.MESH
         )
     in_lse = pltpu.make_async_copy(lse, lv, s_in.at[0])
     in_delta = pltpu.make_async_copy(delta, dv, s_in.at[1])
+    in_listed = pltpu.make_async_copy(listed, lm, s_in.at[2])
     in_lse.start()
     in_delta.start()
+    in_listed.start()
 
     def stats_swap(blk):
         return remote(ms.at[1 - p], st.at[OWN, blk], s_sd.at[0], r_sd.at[0], sib)
 
     pl.semaphore_wait(barrier, len(greeted))
+    for n in range(2):
+        for plane in range(2):
+            for d in range(2):
+                first_query(d, plane, n).start()
+    for n in range(2):
+        for plane in range(2):
+            first_keys(plane, n).start()
     swap_start(queries, 0)
     swap_start(clean, 0)
     in_lse.wait()
     in_delta.wait()
+    in_listed.wait()
     for plane in range(2):
         ms[plane, 0:nh] = lv[plane * nh : (plane + 1) * nh] * LOG2E
         ms[plane, 8 : 8 + nh] = dv[plane * nh : (plane + 1) * nh]
         for n in range(8):
-            ms[plane, 16 + n : 17 + n] = jnp.full((1, BLK), listed[0, n].astype(F32))
+            ms[plane, 16 + n : 17 + n] = jnp.full((1, BLK), lm[0, n].astype(F32))
     st[OWN, p] = ms[p]
     stats_swap(p).start()
-    swap_wait(queries, 0)
-    load(0).send_own()
-    swap_wait(clean, 0)
-    keys_on(0, 0).start()
     stats_swap(1 - p).wait_recv()
     stats.send_own()
     for g in range(1, min(3, nh)):
@@ -396,9 +453,15 @@
         swap_start(clean, g)
     for n in range(4):
         mine_copy(n).start()
-    load(0).relay()
+    for d in range(2):
+        for n in range(2):
+            for core in range(2):
+                first_query_recv(d, core, n).wait_recv()
+    load(0).relay_down().start()
+    load(0).relay_up().start()
     stats.relay()
-    keys_on(1, 0).start()
+    swap_wait(queries, 0)
+    swap_wait(clean, 0)
     if nh > 1:
         swap_wait(queries, 1)
         load(1).send_own()
@@ -432,39 +495,36 @@
             finish_clean(0, t - 1)
             finish_clean(1, t - 1)
 
-        @pl.when(t >= 2)
-        def _():
-            finish(t - 2)
-
         @pl.when(t >= 3)
         def _():
-            drain(t - 3)
+            finish(t - 3)
+
+        @pl.when(t >= 4)
+        def _():
+            drain(t - 4)
 
         return 0
 
     lax.fori_loop(0, nh, step, 0)
-    send_near(nh - 1)
+    for g in range(max(nh - 2, 0), nh):
+        send_near(g)
     finish_clean(0, nh - 1)
+    for g in range(max(nh - 4, 0), nh - 1):
+        if g >= nh - 3:
+            finish(g)
+        drain(g)
+    stats_swap(p).wait_send()
+    stats.done_own()
+    stats.done()
     finish_clean(1, nh - 1)
-    if nh > 1:
-        finish(nh - 2)
     finish(nh - 1)
-
-    stats_swap(p).wait_send()
-    stats.done()
-    for g in range(max(nh - 3, 0), nh):
-        drain(g)
+    drain(nh - 1)
 
 
 def copy_out(*refs):
     sources, results, held, arrive, leave = refs[:5], refs[5:10], refs[10:15], refs[15], refs[16]
-    into, out = [], []
-    for n in range(5):
-        rows = sources[n].shape[0] // 2
-        for k in range(2):
-            span = pl.ds(k * rows, rows)
-            into.append(pltpu.make_async_copy(sources[n].at[span], held[n].at[span], arrive.at[n, k]))
-            out.append(pltpu.make_async_copy(held[n].at[span], results[n].at[span], leave.at[n, k]))
+    into = [pltpu.make_async_copy(sources[n], held[n], arrive.at[n]) for n in range(5)]
+    out = [pltpu.make_async_copy(held[n], results[n], leave.at[n]) for n in range(5)]
     for copy in into:
         copy.start()
     for one, two in zip(into, out, strict=True):
@@ -490,7 +550,7 @@
         vm((4, BLK, width), BF16),
         vm((2 * nh, *tile), F32),
         vm((4, 2, *tile), F32),
-        vm((2, *tile), F32),
+        vm((2, 2, *tile), F32),
         vm((5, 2, CLEAN, HD), F32),
         vm((nh, 2, 2, CLEAN, HD), BF16),
         vm((nh, 2, 2, CLEAN, HD), BF16),
@@ -501,7 +561,8 @@
         vm((nh, *tile), BF16),
         vm((nh, *tile), BF16),
         vm((BLK, width), BF16),
-        dma((2,)),
+        pltpu.SMEM((1, 8), jnp.int32),
+        dma((3,)),
         dma((4,)),
         dma((4, nh)),
         dma((4, nh)),
@@ -510,6 +571,10 @@
         dma((1,)),
         dma((2, nh)),
         dma((2, nh)),
+        dma((2, 2, 2)),
+        dma((2, 2, 2)),
+        dma((2, 2)),
+        dma((2, 2)),
         *[dma((nh + 1,)) for _ in range(6)],
         dma((2, nh + 1)),
         dma((2, nh)),
@@ -531,7 +596,7 @@
         functools.partial(kernel, rows, nh),
         out_shape=[jax.ShapeDtypeStruct((BLK, width), BF16)] * 3
         + [jax.ShapeDtypeStruct((CLEAN, width), BF16)] * 2,
-        in_specs=[hbm] * 8 + [pl.BlockSpec(memory_space=pltpu.SMEM)],
+        in_specs=[hbm] * 9,
         out_specs=[hbm] * 5,
         scratch_shapes=scratch,
         compiler_params=pltpu.CompilerParams(
@@ -549,7 +614,7 @@
         out_shape=[jax.ShapeDtypeStruct(out.shape, out.dtype) for out in outs],
         in_specs=[hbm] * 5,
         out_specs=[hbm] * 5,
-        scratch_shapes=[vm(out.shape, out.dtype) for out in outs] + [dma((5, 2)), dma((5, 2))],
+        scratch_shapes=[vm(out.shape, out.dtype) for out in outs] + [dma((5,)), dma((5,))],
         name="copy_out",
     )(*outs)
 

time: 136 us -> 135 us (level)
  no operation moved by 1% of the time
where the time goes in v3:
time: 135 us
  Pallas kernels  134 us (99%)
    pallas_call x1, Pallas kernels, per_device(): pl.pallas_call(functools.partial(kernel, rows, nh), out_shape=[jax.ShapeD...  128 us
    pallas_call x1, Pallas kernels, per_device(): pl.pallas_call(copy_out, out_shape=[jax.ShapeDtypeStruct(out.shape, out.d...  5.72 us

profile of v3, /device:TPU:1, one launch (start us, length us, event | category | flops | bytes accessed | tf_op | source)
XLA Modules:
  0.0 134.6 jit_solution(14490627231976013930)
XLA Ops:
  0.6 128.2 %block_attention_backward.1 = (bf16[256,2048]{1,0:T(8,128)(2,1)}, bf16[256,2048]{1,0:T(8,128)(2,1)}, bf16[256,2048]{1,0:T(8,128)(2,1)}, bf16[512,2048]{1,0:T(8,128)(2,1)}, bf16[512,2048]{1,0:T(8,128)(2,1)}) custom-call(bf16[256,2048]{1,0:T(8,128)(2,1)} %q.1, bf16[256,2048]{1,0:T(8,128)(2,1)} %do.1, bf16[256,2048]{1,0:T(8,128)(2,1)} %kn.1, ...), custom_call_target="tpu_custom_call" | custom-call | flops 22817013760 | bytes 15728640 | tf_op jit(solution)/shard_map/block_attention_backward/pallas_call | solution.py:595
  128.9 5.7 %copy_out.1 = (bf16[256,2048]{1,0:T(8,128)(2,1)}, bf16[256,2048]{1,0:T(8,128)(2,1)}, bf16[256,2048]{1,0:T(8,128)(2,1)}, bf16[512,2048]{1,0:T(8,128)(2,1)}, bf16[512,2048]{1,0:T(8,128)(2,1)}) custom-call(bf16[256,2048]{1,0:T(8,128)(2,1)} %get-tuple-element.10.refs_0_, bf16[256,2048]{1,0:T(8,128)(2,1)} %get-tuple-element.11.refs_1_, ...), custom_call_target="tpu_custom_call" | custom-call | tf_op jit(solution)/shard_map/copy_out/pallas_call | solution.py:612

commit v4 on v3

--- a/solution.py
+++ b/solution.py
@@ -453,6 +453,9 @@
         swap_start(clean, g)
     for n in range(4):
         mine_copy(n).start()
+    for n in range(4):
+        mine_copy(n).wait()
+    own_pairs(0)
     for d in range(2):
         for n in range(2):
             for core in range(2):
@@ -477,12 +480,9 @@
 
         first_half(t)
 
-        @pl.when(t == 0)
-        def _():
-            for n in range(4):
-                mine_copy(n).wait()
-
-        own_pairs(t)
+        @pl.when(t + 1 < nh)
+        def _():
+            own_pairs(t + 1)
 
         @pl.when(t + 1 < nh)
         def _():

time: 135 us -> 134 us (level)
  no operation moved by 1% of the time
where the time goes in v4:
time: 134 us
  Pallas kernels  133 us (99%)
    pallas_call x1, Pallas kernels, per_device(): pl.pallas_call(functools.partial(kernel, rows, nh), out_shape=[jax.ShapeD...  127 us
    pallas_call x1, Pallas kernels, per_device(): pl.pallas_call(copy_out, out_shape=[jax.ShapeDtypeStruct(out.shape, out.d...  5.72 us

profile of v4, /device:TPU:1, one launch (start us, length us, event | category | flops | bytes accessed | tf_op | source)
XLA Modules:
  0.0 133.6 jit_solution(11391027704859141186)
XLA Ops:
  0.6 127.3 %block_attention_backward.1 = (bf16[256,2048]{1,0:T(8,128)(2,1)}, bf16[256,2048]{1,0:T(8,128)(2,1)}, bf16[256,2048]{1,0:T(8,128)(2,1)}, bf16[512,2048]{1,0:T(8,128)(2,1)}, bf16[512,2048]{1,0:T(8,128)(2,1)}) custom-call(bf16[256,2048]{1,0:T(8,128)(2,1)} %q.1, bf16[256,2048]{1,0:T(8,128)(2,1)} %do.1, bf16[256,2048]{1,0:T(8,128)(2,1)} %kn.1, ...), custom_call_target="tpu_custom_call" | custom-call | flops 22817013760 | bytes 15728640 | tf_op jit(solution)/shard_map/block_attention_backward/pallas_call | solution.py:595
  127.9 5.7 %copy_out.1 = (bf16[256,2048]{1,0:T(8,128)(2,1)}, bf16[256,2048]{1,0:T(8,128)(2,1)}, bf16[256,2048]{1,0:T(8,128)(2,1)}, bf16[512,2048]{1,0:T(8,128)(2,1)}, bf16[512,2048]{1,0:T(8,128)(2,1)}) custom-call(bf16[256,2048]{1,0:T(8,128)(2,1)} %get-tuple-element.10.refs_0_, bf16[256,2048]{1,0:T(8,128)(2,1)} %get-tuple-element.11.refs_1_, ...), custom_call_target="tpu_custom_call" | custom-call | tf_op jit(solution)/shard_map/copy_out/pallas_call | solution.py:612
